TPU v7x, 32 devices: a whole 2x2x4 slice. The times are simulated.
32 devices in a mesh: rows: 8 (over z, y), heads: 4 (over x, core).
Axes of the slice: x: 2, y: 2, z: 4, core: 2. Of those that a mesh axis runs over, the one named last changes fastest.
Arguments:
- tokens: bfloat16 [24576, 768], P(('rows', 'heads')), may hold values from -6 to 6
- lengths: int32 [24, 24], P('rows'), may hold values from 1 to 512, 1024 in all within a row
- w_query: bfloat16 [768, 768], P(None, 'heads'), may hold values from -0.21875 to 0.21875
- w_key: bfloat16 [768, 768], P(None, 'heads'), may hold values from -0.21875 to 0.21875
- w_value: bfloat16 [768, 768], P(None, 'heads'), may hold values from -0.21875 to 0.21875
- w_out: bfloat16 [768, 768], P('heads'), may hold values from -0.625 to 0.625
- w_up: bfloat16 [768, 3072], P(None, 'heads'), may hold values from -0.21875 to 0.21875
- w_down: bfloat16 [3072, 768], P('heads'), may hold values from -0.109375 to 0.109375
- gain_first: bfloat16 [768], P('heads'), may hold values from 0.5 to 1.5
- shift_first: bfloat16 [768], P('heads'), may hold values from -3 to 3
- gain_second: bfloat16 [768], P('heads'), may hold values from 0.5 to 1.5
- shift_second: bfloat16 [768], P('heads'), may hold values from -3 to 3
- cotangent: bfloat16 [24576, 768], P(('rows', 'heads')), may hold values from -6 to 6
Outputs:
- mixed: bfloat16 [24576, 768], P(('rows', 'heads'))
- grad_tokens: float32 [24576, 768], P(('rows', 'heads'))
- grad_query: float32 [768, 768], P(None, 'heads')
- grad_key: float32 [768, 768], P(None, 'heads')
- grad_value: float32 [768, 768], P(None, 'heads')
- grad_out: float32 [768, 768], P('heads')
- grad_up: float32 [768, 3072], P(None, 'heads')
- grad_down: float32 [3072, 768], P('heads')
- grad_gain_first: float32 [768], P('heads')
- grad_shift_first: float32 [768], P('heads')
- grad_gain_second: float32 [768], P('heads')
- grad_shift_second: float32 [768], P('heads')
Inputs may be any that keep to these rules, and one draw needn't show every extreme that they name: `lengths`: each packed row of 1024 tokens is filled exactly by its 24 documents, and every row holds one document of exactly 512 tokens.
All inputs are finite; a program needn't handle non-finite values.
Results may differ from a plain program's by a relative error of at most 0.013.
Values may be sent and summed in bfloat16 or wider, within the bound.
A program may use at most 128 MiB of HBM per device.

v0:
```python
import jax
import jax.numpy as jnp
from jax import lax
from jax.sharding import PartitionSpec as P

HEAD_WIDTH = 64


norm_eps = 1e-12


def layer_norm(values, gain, shift):
    centre = jnp.mean(values, axis=-1, keepdims=True)
    centred = values - centre
    spread = jnp.mean(centred * centred, axis=-1, keepdims=True)
    return centred * lax.rsqrt(spread + norm_eps) * gain + shift


def gelu_exact(values):
    return jax.nn.gelu(values, approximate=False)


def contract_last(left, right):
    return lax.dot_general(
        left, right, (((1,), (1,)), ((), ())), preferred_element_type=jnp.float32
    )


def contract_first(left, right):
    return lax.dot_general(
        left, right, (((0,), (0,)), ((), ())), preferred_element_type=jnp.float32
    )


def local(
    tokens,
    lengths,
    w_query,
    w_key,
    w_value,
    w_out,
    w_up,
    w_down,
    gain_first,
    shift_first,
    gain_second,
    shift_second,
    cotangent,
):
    bf16 = jnp.bfloat16
    f32 = jnp.float32
    packed_rows = lengths.shape[0]
    width = tokens.shape[1]
    own_rows = tokens.shape[0]
    width_dev = w_query.shape[1]
    heads_per_device = width_dev // HEAD_WIDTH
    scaling = float(HEAD_WIDTH) ** (-0.5)
    group_tok = lax.all_gather(tokens, "heads", axis=0, tiled=True)
    group_length = group_tok.shape[0]
    row_length = group_length // packed_rows
    out_full, up_full, down_full, gain_one, shift_one, gain_two, shift_two = (
        lax.all_gather(w_out, "heads", axis=0, tiled=True),
        lax.all_gather(w_up, "heads", axis=1, tiled=True),
        lax.all_gather(w_down, "heads", axis=0, tiled=True),
        lax.all_gather(gain_first, "heads", axis=0, tiled=True),
        lax.all_gather(shift_first, "heads", axis=0, tiled=True),
        lax.all_gather(gain_second, "heads", axis=0, tiled=True),
        lax.all_gather(shift_second, "heads", axis=0, tiled=True),
    )
    doc_ends = jnp.cumsum(lengths, axis=1)
    token_position = lax.broadcasted_iota(jnp.int32, (packed_rows, row_length, lengths.shape[1]), 1)
    document_span = jnp.sum((token_position >= doc_ends[:, None, :]).astype(jnp.int32), axis=2)
    query_all = jnp.dot(group_tok, w_query, preferred_element_type=f32).astype(bf16)
    key_all = jnp.dot(group_tok, w_key, preferred_element_type=f32).astype(bf16)
    value_all = jnp.dot(group_tok, w_value, preferred_element_type=f32).astype(bf16)

    def rows_view(values_array):
        return values_array.reshape(packed_rows, row_length, heads_per_device, HEAD_WIDTH)

    def row_scores(query_row, key_row, seg_row):
        same_doc = seg_row[:, None] == seg_row[None, :]
        scores = (
            jnp.einsum("qhe,khe->hqk", query_row, key_row, preferred_element_type=f32) * scaling
        )
        return jnp.where(same_doc[None], scores, -1e30)

    def forward_row(pieces):
        query_row, key_row, value_row, seg_row = pieces
        scores = row_scores(query_row, key_row, seg_row)
        row_max = jnp.max(scores, axis=2, keepdims=True)
        exp_terms = jnp.exp(scores - row_max)
        row_total = jnp.sum(exp_terms, axis=2, keepdims=True)
        attn_probs = (exp_terms / row_total).astype(bf16)
        context_row = jnp.einsum("hqk,khe->qhe", attn_probs, value_row, preferred_element_type=f32)
        return (context_row.astype(bf16), (row_max + jnp.log(row_total))[..., 0])

    context, logsum = lax.map(
        forward_row, (rows_view(query_all), rows_view(key_all), rows_view(value_all), document_span)
    )
    context_tok = lax.all_to_all(
        context.reshape(group_length, width_dev), "heads", split_axis=0, concat_axis=1, tiled=True
    )
    attn_out = jnp.dot(context_tok, out_full, preferred_element_type=f32)
    resid = tokens.astype(f32) + attn_out
    hidden, norm_one_back = jax.vjp(layer_norm, resid, gain_one.astype(f32), shift_one.astype(f32))
    hidden_low = hidden.astype(bf16)
    up_proj = jnp.dot(hidden_low, up_full, preferred_element_type=f32)
    active, gelu_back = jax.vjp(gelu_exact, up_proj)
    active_low = active.astype(bf16)
    ffn_out = jnp.dot(active_low, down_full, preferred_element_type=f32)
    normed, norm_two_back = jax.vjp(
        layer_norm, hidden + ffn_out, gain_two.astype(f32), shift_two.astype(f32)
    )
    mixed = normed.astype(bf16)
    grad_total, grad_gain_two, grad_shift_two = norm_two_back(cotangent.astype(f32))
    grad_ffn = grad_total.astype(bf16)
    grad_down = contract_first(active_low, grad_ffn)
    grad_active = contract_last(grad_ffn, down_full)
    grad_upproj = gelu_back(grad_active)[0].astype(bf16)
    grad_up = contract_first(hidden_low, grad_upproj)
    grad_hidden = grad_total + contract_last(grad_upproj, up_full)
    grad_resid, grad_gain_one, grad_shift_one = norm_one_back(grad_hidden)
    grad_attn = grad_resid.astype(bf16)
    grad_out = contract_first(context_tok, grad_attn)
    grad_context = contract_last(grad_attn, out_full).astype(bf16)
    grad_context_heads = lax.all_to_all(
        grad_context, "heads", split_axis=1, concat_axis=0, tiled=True
    )

    def backward_row(pieces):
        query_row, key_row, value_row, seg_row, lse_row, grad_ctx_row = pieces
        scores = row_scores(query_row, key_row, seg_row)
        attn_probs = jnp.exp(scores - lse_row[..., None])
        grad_value_row = jnp.einsum(
            "hqk,qhe->khe", attn_probs.astype(bf16), grad_ctx_row, preferred_element_type=f32
        )
        grad_probs = jnp.einsum("qhe,khe->hqk", grad_ctx_row, value_row, preferred_element_type=f32)
        row_delta = jnp.sum(attn_probs * grad_probs, axis=2, keepdims=True)
        grad_scores = (attn_probs * (grad_probs - row_delta)).astype(bf16)
        grad_query_row = (
            jnp.einsum("hqk,khe->qhe", grad_scores, key_row, preferred_element_type=f32) * scaling
        )
        grad_key_row = (
            jnp.einsum("hqk,qhe->khe", grad_scores, query_row, preferred_element_type=f32) * scaling
        )
        return (grad_query_row.astype(bf16), grad_key_row.astype(bf16), grad_value_row.astype(bf16))

    grad_q_rows, grad_k_rows, grad_v_rows = lax.map(
        backward_row,
        (
            rows_view(query_all),
            rows_view(key_all),
            rows_view(value_all),
            document_span,
            logsum,
            rows_view(grad_context_heads),
        ),
    )
    grad_qproj = grad_q_rows.reshape(group_length, width_dev)
    grad_kproj = grad_k_rows.reshape(group_length, width_dev)
    grad_vproj = grad_v_rows.reshape(group_length, width_dev)
    grad_query = contract_first(group_tok, grad_qproj)
    grad_key = contract_first(group_tok, grad_kproj)
    grad_value = contract_first(group_tok, grad_vproj)
    term_sum = jnp.zeros((lax.axis_size("heads") * own_rows, width), f32)
    for grad_part, weight_part in (
        (grad_qproj, w_query),
        (grad_kproj, w_key),
        (grad_vproj, w_value),
    ):
        term_sum = term_sum + contract_last(grad_part, weight_part)
    grad_from_proj = lax.psum_scatter(term_sum, "heads", scatter_dimension=0, tiled=True)
    grad_tokens = grad_resid + grad_from_proj
    part_out, part_up, part_down, part_gain_one, part_shift_one, part_gain_two, part_shift_two = (
        lax.psum_scatter(grad_out, "heads", scatter_dimension=0, tiled=True),
        lax.psum_scatter(grad_up, "heads", scatter_dimension=1, tiled=True),
        lax.psum_scatter(grad_down, "heads", scatter_dimension=0, tiled=True),
        lax.psum_scatter(grad_gain_one, "heads", scatter_dimension=0, tiled=True),
        lax.psum_scatter(grad_shift_one, "heads", scatter_dimension=0, tiled=True),
        lax.psum_scatter(grad_gain_two, "heads", scatter_dimension=0, tiled=True),
        lax.psum_scatter(grad_shift_two, "heads", scatter_dimension=0, tiled=True),
    )
    summed = lax.psum(
        (
            grad_query,
            grad_key,
            grad_value,
            part_out,
            part_up,
            part_down,
            part_gain_one,
            part_shift_one,
            part_gain_two,
            part_shift_two,
        ),
        "rows",
    )
    return (
        mixed,
        grad_tokens,
        summed[0],
        summed[1],
        summed[2],
        summed[3],
        summed[4],
        summed[5],
        summed[6],
        summed[7],
        summed[8],
        summed[9],
    )


def solution(mesh):
    placed = (
        P(("rows", "heads"), None),
        P("rows", None),
        P(None, "heads"),
        P(None, "heads"),
        P(None, "heads"),
        P("heads", None),
        P(None, "heads"),
        P("heads", None),
        P("heads"),
        P("heads"),
        P("heads"),
        P("heads"),
        P(("rows", "heads"), None),
    )
    return jax.shard_map(
        local,
        mesh=mesh,
        in_specs=placed,
        out_specs=(
            P(("rows", "heads"), None),
            P(("rows", "heads"), None),
            P(None, "heads"),
            P(None, "heads"),
            P(None, "heads"),
            P("heads", None),
            P(None, "heads"),
            P("heads", None),
            P("heads"),
            P("heads"),
            P("heads"),
            P("heads"),
        ),
        check_vma=False,
    )
```

profile of v0, /device:TPU:0, one launch (start us, length us, event | category | flops | bytes accessed | tf_op | source)
XLA Modules:
  0.0 762.5 jit_solution(14402335155313762133)
XLA Ops:
  9.8 40.0 %all-gather.5.cloned.1.call-done = bf16[3072,768]{1,0:T(8,128)(2,1)} async-done(((bf16[768,768]{1,0:T(8,128)(2,1)}), bf16[3072,768]{1,0:T(8,128)(2,1)}) %all-gather.5.cloned.1.call-update) | async-done | bytes 4718608 | tf_op jit(solution)/shard_map/all_gather | solution.py:58
  57.1 4.3 convolution_convert_fusion.2
  73.1 43.7 %while.26 = (s32[]{:T(128)}, bf16[3,1024,3,64]{1,3,2,0:T(8,128)(2,1)}, f32[3,3,1024]{2,1,0:T(4,128)S(1)}, bf16[3,1024,3,64]{1,3,2,0:T(8,128)(2,1)}, s32[3,1024]{...) while((s32[]{:T(128)}, ...), condition=%wide.region_5.6_spmd, body=%wide.region_2.5_spmd.sunk | while | flops 844297216 | bytes 47835256 | solution.py:97
  82.0 5.7 fusion.139
  96.6 5.7 fusion.139
  111.1 5.7 fusion.139
  121.4 4.8 all-to-all-start
  130.6 15.4 %all-reduce.11 = (bf16[768]{0:T(1024)(128)(2,1)S(1)}, bf16[768]{0:T(1024)(128)(2,1)S(1)}, bf16[768]{0:T(1024)(128)(2,1)S(1)}, bf16[768]{0:T(1024)(128)(2,1)S(1)}) all-reduce(bf16[768]{0:T(1024)(128)(2,1)S(1)} %dynamic-update-slice.1, bf16[768]{0:T(1024)(128)(2,1)S(1)} %dynamic-update-slice, ...), channel_id=1, replica_groups=mesh['rows'=8,'heads'=4] {'heads'}, use_global_device_ids=true, to_apply=%add.1 | all-reduce | flops 3072 | bytes 12288
  151.7 29.6 %multiply_convert_fusion.1 = (bf16[768,3072]{1,0:T(8,128)(2,1)}, f32[768,3072]{1,0:T(8,128)}, f32[768,3072]{1,0:T(8,128)}) fusion(bf16[768,3072]{1,0:T(8,128)(2,1)} %all-gather.9.cloned.1.call-done, f32[768,768]{0,1:T(8,128)} %copy-done.8, f32[768]{0:T(1024)S(1)} %convert_element_type.90, f32[768]{0:T(1024)S(1)} %convert_element_type.89, ...), kind=kOutput, calls=%fused_computation.70 | convolution fusion | flops 3780182016 | bytes 30683136 | tf_op jit(solution)/shard_map/dot_general | solution.py:107
  181.3 8.9 %fusion.85 = (f32[768]{0:T(1024)S(1)}, f32[768,768]{0,1:T(8,128)S(1)}) fusion(bf16[768,3072]{1,0:T(8,128)(2,1)} %get-tuple-element.287, bf16[3072,768]{1,0:T(8,128)(2,1)} %all-gather.11.cloned.1.call-done, f32[768]{0:T(1024)S(1)} %convert_element_type.90, f32[768]{0:T(1024)S(1)} %convert_element_type.89, f32[768]{0:T(1024)S(1)} %fusion.74, ...), kind=kOutput, calls=%fused_computation.134 | convolution fusion | flops 3627416832 | bytes 14171136 | tf_op jit(solution)/shard_map/dot_general | solution.py:110
  194.6 13.5 %add_convert_fusion = bf16[768,3072]{1,0:T(8,128)(2,1)} fusion(f32[768,3072]{1,0:T(8,128)} %get-tuple-element.288, f32[768,3072]{1,0:T(8,128)} %get-tuple-element.300, bf16[3072,768]{1,0:T(8,128)(2,1)} %all-gather.11.cloned.1.call-done, f32[768]{0:T(1024)S(1)} %negate_multiply_fusion.2, bf16[768,768]{0,1:T(8,128)(2,1)S(1)} %copy.103, ...), kind=kOutput, calls=%fused_computation.69 | convolution fusion | flops 3662217216 | bytes 31865856 | tf_op jit(solution)/shard_map/dot_general | solution.py:24
  208.2 9.2 %multiply_reduce_fusion.1 = (f32[768]{0:T(1024)}, f32[768]{0:T(1024)S(1)}, f32[768]{0:T(1024)}, f32[768,768]{0,1:T(8,128)S(1)}) fusion(f32[768,768]{0,1:T(8,128)S(1)} %copy-done.9, f32[768]{0:T(1024)S(1)} %fusion.74, f32[768]{0:T(1024)S(1)} %broadcast_multiply_fusion.1, f32[768]{0:T(1024)S(1)} %convert_element_type.89, ...), kind=kOutput, calls=%fused_computation.96 | convolution fusion | flops 3633903360 | bytes 17728512 | tf_op jit(solution)/shard_map/dot_general | solution.py:24
  223.4 11.4 %fusion.71 = f32[3072,768]{1,0:T(8,128)} fusion(bf16[768,3072]{1,0:T(8,128)(2,1)} %get-tuple-element.287, f32[768]{0:T(1024)S(1)} %negate_multiply_fusion.2, bf16[768,768]{0,1:T(8,128)(2,1)S(1)} %copy.103, f32[768,768]{0,1:T(8,128)} %copy-done.11, f32[768]{0:T(1024)S(1)} %get-tuple-element.294, f32[768]{0:T(1024)S(1)} %convert_element_type.93, ...), kind=kOutput, calls=%fused_computation.113 | convolution fusion | flops 3629187072 | bytes 17710080 | tf_op jit(solution)/shard_map/dot_general | solution.py:30
  236.4 8.9 %fusion.76 = f32[768,3072]{1,0:T(8,128)} fusion(bf16[768,3072]{1,0:T(8,128)(2,1)} %add_convert_fusion, f32[768,768]{0,1:T(8,128)S(1)} %copy-done.10, f32[768]{0:T(1024)S(1)} %convert_element_type.90, f32[768]{0:T(1024)S(1)} %convert_element_type.89, f32[768]{0:T(1024)S(1)} %fusion.74, f32[768]{0:T(1024)S(1)} %broadcast_multiply_fusion.1), kind=kOutput, calls=%fused_computation.128 | convolution fusion | flops 3626827776 | bytes 16527360 | tf_op jit(solution)/shard_map/dot_general | solution.py:30
  249.3 19.8 %all_to_all.35 = bf16[768,4,192]{0,2,1:T(8,128)(2,1)S(1)} all-to-all(bf16[768,4,192]{0,2,1:T(8,128)(2,1)S(1)} %bitcast.185), channel_id=1, replica_groups=mesh['rows'=8,'heads'=4] {'heads'}, dimensions={1} | all-to-all | bytes 2359296 | tf_op jit(solution)/shard_map/all_to_all | solution.py:126
  275.9 84.3 %while.27 = (s32[]{:T(128)}, bf16[3,1024,3,64]{1,3,2,0:T(8,128)(2,1)}, bf16[3,1024,3,64]{1,3,2,0:T(8,128)(2,1)}, bf16[3,1024,3,64]{1,3,2,0:T(8,128)(2,1)}, bf16[...) while((s32[]{:T(128)}, ...), condition=%wide.region_16.17_spmd, body=%wide.region_14.16_spmd.sunk | while | flops 2062480384 | bytes 102601840 | solution.py:148
  278.4 8.3 %multiply_reduce_fusion.6 = (f32[3,1024]{1,0:T(4,128)S(1)}, f32[3,1024,1024]{1,2,0:T(8,128)}) fusion(f32[3,1024,1024]{1,2,0:T(8,128)S(1)} %fusion.148, f32[3,1024]{1,0:T(4,128)S(1)} %dynamic-slice_bitcast_fusion.2, pred[1024,1024]{0,1:T(8,128)(4,1)S(1)} %broadcast_compare_fusion.5, bf16[3,1024,3,64]{1,3,2,0:T(8,128)(2,1)} %get-tuple-element.471, ...), kind=kOutput, calls=%fused_computation.24.clone.1 | convolution fusion | flops 418378752 | bytes 27026432 | tf_op jit(solution)/shard_map/while/body/eval_jaxpr/qhe,khe->hqk/dot_general | solution.py:137
  286.7 6.9 multiply_convert_fusion.3
  298.4 5.4 fusion.151
  306.4 8.3 %multiply_reduce_fusion.6 = (f32[3,1024]{1,0:T(4,128)S(1)}, f32[3,1024,1024]{1,2,0:T(8,128)}) fusion(f32[3,1024,1024]{1,2,0:T(8,128)S(1)} %fusion.148, f32[3,1024]{1,0:T(4,128)S(1)} %dynamic-slice_bitcast_fusion.2, pred[1024,1024]{0,1:T(8,128)(4,1)S(1)} %broadcast_compare_fusion.5, bf16[3,1024,3,64]{1,3,2,0:T(8,128)(2,1)} %get-tuple-element.471, ...), kind=kOutput, calls=%fused_computation.24.clone.1 | convolution fusion | flops 418378752 | bytes 27026432 | tf_op jit(solution)/shard_map/while/body/eval_jaxpr/qhe,khe->hqk/dot_general | solution.py:137
  314.6 7.0 multiply_convert_fusion.3
  326.5 5.4 fusion.151
  334.4 8.3 %multiply_reduce_fusion.6 = (f32[3,1024]{1,0:T(4,128)S(1)}, f32[3,1024,1024]{1,2,0:T(8,128)}) fusion(f32[3,1024,1024]{1,2,0:T(8,128)S(1)} %fusion.148, f32[3,1024]{1,0:T(4,128)S(1)} %dynamic-slice_bitcast_fusion.2, pred[1024,1024]{0,1:T(8,128)(4,1)S(1)} %broadcast_compare_fusion.5, bf16[3,1024,3,64]{1,3,2,0:T(8,128)(2,1)} %get-tuple-element.471, ...), kind=kOutput, calls=%fused_computation.24.clone.1 | convolution fusion | flops 418378752 | bytes 27026432 | tf_op jit(solution)/shard_map/while/body/eval_jaxpr/qhe,khe->hqk/dot_general | solution.py:137
  342.6 7.1 multiply_convert_fusion.3
  354.5 5.5 fusion.151
  369.4 5.1 add_add_fusion
  374.5 4.7 convolution_bitcast_fusion
  387.7 33.4 %reduce-scatter.9.cloned.1.call-done = f32[768,768]{1,0:T(8,128)} async-done(((f32[768,3072]{1,0:T(8,128)}), f32[768,768]{1,0:T(8,128)}) %reduce-scatter.9.cloned.1.call-update) | async-done | bytes 2359312 | tf_op jit(solution)/shard_map/reduce_scatter | solution.py:176
  422.0 10.1 %all-reduce.10 = (f32[768]{0:T(1024)S(1)}, f32[768]{0:T(1024)S(1)}, f32[768]{0:T(1024)S(1)}, f32[768]{0:T(1024)S(1)}) all-reduce(f32[768]{0:T(1024)S(1)} %copy-done.28, f32[768]{0:T(1024)S(1)} %copy-done.29, f32[768]{0:T(1024)S(1)} %copy-done.27, f32[768]{0:T(1024)S(1)} %copy-done.26), channel_id=6, replica_groups=mesh['rows'=8,'heads'=4] {'heads'}, use_global_device_ids=true, to_apply=%region_28.29.clone | all-reduce | flops 3072 | bytes 24576
  435.0 22.0 %all-reduce.8 = (f32[192]{0:T(256)}, f32[192]{0:T(256)}, f32[192]{0:T(256)}, f32[192]{0:T(256)}) all-reduce(f32[192]{0:T(256)S(1)} %dynamic-slice.5, f32[192]{0:T(256)S(1)} %dynamic-slice.7, f32[192]{0:T(256)S(1)} %dynamic-slice.9, f32[192]{0:T(256)S(1)} %dynamic-slice.11), channel_id=1, replica_groups=mesh['rows'=8,'heads'=4] {'rows'}, use_global_device_ids=true, to_apply=%region_29.30 | all-reduce | flops 768 | bytes 6144 | tf_op jit(solution)/shard_map/psum | solution.py:183
  457.0 45.4 %reduce-scatter.5.cloned.1.call-done = f32[768,768]{0,1:T(8,128)} async-done(((f32[3072,768]{0,1:T(8,128)}), f32[768,768]{0,1:T(8,128)}) %reduce-scatter.5.cloned.1.call-update) | async-done | bytes 2359312 | tf_op jit(solution)/shard_map/reduce_scatter | solution.py:172
  508.8 237.5 %all-reduce.14.cloned.1.call-done = (f32[768,192]{0,1:T(8,128)}, f32[768,192]{0,1:T(8,128)}, f32[768,192]{0,1:T(8,128)}, f32[192,768]{1,0:T(8,128)}, f32[768,768]{1,0:T(8,128)}, /*index=5*/f32[768,768]{1,0:T(8,128)}) async-done(((f32[768,192]{0,1:T(8,128)}, f32[768,192]{0,1:T(8,128)}, f32[768,192]{0,1:T(8,128)}, f32[192,768]{1,0:T(8,128)}, f32[768,768]{1,0:T(8,128)}, /*index=5*/f32[768,768]{1,0:T(8,128)}), ...) | async-done | bytes 7077904 | tf_op jit(solution)/shard_map/psum | solution.py:183
  (206 shorter events, 142.8 us)
Async XLA Ops:
  7.2 57.5 %copy-start = (bf16[768,192]{0,1:T(8,128)(2,1)S(1)}, bf16[768,192]{0,1:T(8,128)(2,1)}, u32[]{:S(2)}) copy-start(bf16[768,192]{0,1:T(8,128)(2,1)} %param.19) | copy-start | bytes 884740
  7.2 42.6 %copy-start.20 = (bf16[768,192]{0,1:T(8,128)(2,1)S(1)}, bf16[768,192]{0,1:T(8,128)(2,1)}, u32[]{:S(2)}) copy-start(bf16[768,192]{0,1:T(8,128)(2,1)} %param.20) | copy-start | bytes 884740
  7.2 42.6 %all-gather.5.cloned.1.call-start = ((), (), s32[]{:S(2)}) async-start(), calls=%async_computation.6 | async-start | bytes 5898240 | tf_op jit(solution)/shard_map/all_gather | solution.py:58
  7.9 138.8 %all-gather.7.cloned.1.call-start = ((), (), s32[]{:S(2)}) async-start(), calls=%async_computation.7 | async-start | bytes 1474560 | tf_op jit(solution)/shard_map/all_gather | solution.py:62
  8.7 143.0 %all-gather.9.cloned.1.call-start = ((), (), s32[]{:S(2)}) async-start(), calls=%async_computation.8 | async-start | bytes 5898240 | tf_op jit(solution)/shard_map/all_gather | solution.py:63
  73.8 4.3 copy-start.1
  88.4 4.3 copy-start.1
  102.9 4.3 copy-start.1
  121.4 5.5 copy-start.12
  121.4 25.3 %all-to-all-start = ((bf16[4,768,192]{1,2,0:T(8,128)(2,1)}), bf16[4,768,192]{1,2,0:T(8,128)(2,1)}, u32[]{:S(2)}, u32[]{:S(2)}) async-start(bf16[4,768,192]{1,2,0:T(8,128)(2,1)} %copy.102), calls=%async_computation | async-start | bytes 2359296 | tf_op jit(solution)/shard_map/all_to_all | solution.py:100
  126.2 3.4 copy-start.32
  126.2 3.6 copy-start.33
  126.2 3.9 copy-start.34
  126.3 4.1 copy-start.35
  126.3 19.8 %copy-start.17 = (bf16[768,768]{1,0:T(8,128)(2,1)S(1)}, bf16[768,768]{1,0:T(8,128)(2,1)}, u32[]{:S(2)}) copy-start(bf16[768,768]{1,0:T(8,128)(2,1)} %param.29) | copy-start | bytes 3538948
  126.3 55.0 %all-gather.11.cloned.1.call-start = ((), (), s32[]{:S(2)}) async-start(), calls=%async_computation.9 | async-start | bytes 5898240 | tf_op jit(solution)/shard_map/all_gather | solution.py:64
  126.9 260.9 %reduce-scatter.7.cloned.1.call-start = ((), (), s32[]{:S(2)}) async-start(), calls=%async_computation.11 | async-start | bytes 2949120 | tf_op jit(solution)/shard_map/reduce_scatter | solution.py:175
  190.2 17.9 %copy-start.11 = (f32[768,768]{0,1:T(8,128)}, f32[768,768]{0,1:T(8,128)S(1)}, u32[]{:S(2)}) copy-start(f32[768,768]{0,1:T(8,128)S(1)} %get-tuple-element.302) | copy-start | bytes 7077892
  194.6 13.5 %copy-start.9 = (f32[768,768]{0,1:T(8,128)S(1)}, f32[768,768]{0,1:T(8,128)}, u32[]{:S(2)}) copy-start(f32[768,768]{0,1:T(8,128)} %copy-done.8) | copy-start | bytes 7077892
  218.1 27.3 %copy-start.24 = (f32[768]{0:T(1024)}, f32[768]{0:T(1024)S(1)}, u32[]{:S(2)}) copy-start(f32[768]{0:T(1024)S(1)} %negate_multiply_fusion.1) | copy-start | bytes 9220
  223.3 164.4 %reduce-scatter.11.cloned.1.call-start = ((), (), s32[]{:S(2)}) async-start(), calls=%async_computation.13 | async-start | bytes 11796480 | tf_op jit(solution)/shard_map/reduce_scatter | solution.py:177
  234.8 186.3 %reduce-scatter.9.cloned.1.call-start = ((), (), s32[]{:S(2)}) async-start(), calls=%async_computation.12 | async-start | bytes 11796480 | tf_op jit(solution)/shard_map/reduce_scatter | solution.py:176
  245.3 257.0 %reduce-scatter.5.cloned.1.call-start = ((), (), s32[]{:S(2)}) async-start(), calls=%async_computation.10 | async-start | bytes 11796480 | tf_op jit(solution)/shard_map/reduce_scatter | solution.py:172
  272.4 3.5 copy-start.2
  272.4 3.5 copy-start.3
  363.1 6.2 copy-start.4
  374.5 371.8 %all-reduce.14.cloned.1.call-start = ((), (), s32[]{:S(2)}) async-start(), calls=%async_computation.14 | async-start | bytes 14155776 | tf_op jit(solution)/shard_map/psum | solution.py:183
  421.2 81.2 %copy-start.7 = (f32[768,768]{0,1:T(8,128)S(1)}, f32[768,768]{0,1:T(8,128)}, u32[]{:S(2)}) copy-start(f32[768,768]{0,1:T(8,128)} %copy-done.5) | copy-start | bytes 7077892
  421.2 81.2 %copy-start.25 = (f32[768]{0:T(1024)S(1)}, f32[768]{0:T(1024)}, u32[]{:S(2)}) copy-start(f32[768]{0:T(1024)} %copy-done.24) | copy-start | bytes 9220
  746.3 4.0 copy-start.19
  746.3 4.8 copy-start.18
  746.3 5.6 copy-start.16
  (16 other events, 27.4 us)
Sparse Core Ops, SparseCore 0:
  9.6 40.1 all-gather.4
  51.4 17.4 all-gather.6
  70.4 37.4 all-gather.8
  128.4 40.7 all-gather.10
  223.5 34.8 reduce-scatter.6
  261.0 78.9 reduce-scatter.10
  342.7 78.3 reduce-scatter.8
  423.9 78.4 reduce-scatter.4
  508.8 237.3 all-reduce.13
where the time goes:
time: 773 us; the launch traced here: 763 us
  waiting for transfers between devices  359 us (46%)
  matrix products  215 us (28%)
  blocking collectives  67.4 us (9%)
  local copies, waits for them, and re-layouts  53.7 us (7%)
  other arithmetic  45.8 us (6%)
  between operations  16.1 us (2%)
    psum x1, waiting for transfers between devices, local(): lax.psum((grad_query, grad_key, grad_value, part_out, part_up, part_down,...  237 us
    reduce_scatter x1, waiting for transfers between devices, local(): lax.psum_scatter(term_sum, 'heads', scatter_dimension=0, tiled=True)  45.4 us
    all_gather x1, waiting for transfers between devices, local(): group_tok = lax.all_gather(tokens, 'heads', axis=0, tiled=True)  40 us
    dot_general x6, matrix products, contract_first(): lax.dot_general(left, right, (((0,), (0,)), ((), ())), preferred_element_...  37.2 us
    reduce_scatter x1, waiting for transfers between devices, local(): lax.psum_scatter(grad_up, 'heads', scatter_dimension=1, tiled=True)  33.4 us
    dot_general x6, matrix products, contract_last(): lax.dot_general(left, right, (((1,), (1,)), ((), ())), preferred_element_...  33.1 us
    dot_general x1, matrix products, local(): up_proj = jnp.dot(hidden_low, up_full, preferred_element_type=f32)  29.6 us
    unnamed x96, local copies, waits for them, and re-layouts  26.9 us
  transfers between devices with their start and end apart: 10, of which 4 were waited for; matrix products, arithmetic and copies ran while one was open for 34% of the time, Pallas kernels for 0%

commit v1 on v0

v1 whole, which is shorter than its diff:
```python
import functools

import jax
import jax.numpy as jnp
from jax import lax
from jax.experimental import pallas as pl
from jax.experimental.pallas import tpu as pltpu
from jax.sharding import PartitionSpec as P

MESH = pl.DeviceIdType.MESH
BF = jnp.bfloat16
F32 = jnp.float32
HEAD_WIDTH = 64
LONGEST_DOC = 512
BLK = 256
HALO = LONGEST_DOC // BLK
NORM_EPS = 1e-12
VMEM_LIMIT = 60 * 1024 * 1024


def nt(left, right):
    return lax.dot_general(left, right, (((1,), (1,)), ((), ())), preferred_element_type=F32)


def nn(left, right):
    return lax.dot_general(left, right, (((1,), (0,)), ((), ())), preferred_element_type=F32)


def flip(index, bit):
    return index + bit - 2 * bit * ((index // bit) % 2)


def place():
    r, h = lax.axis_index("rows"), lax.axis_index("heads")
    return r, h


def greet(ids):
    barrier = pltpu.get_barrier_semaphore()
    for who in ids:
        pl.semaphore_signal(barrier, inc=1, device_id=who, device_id_type=MESH)
    pl.semaphore_wait(barrier, len(ids))


def group_of(r, h, groups):
    return [(r, lax.rem(h + i, groups)) for i in range(1, groups)]


def remote(src, dst, send, recv, who):
    return pltpu.make_async_remote_copy(
        src_ref=src, dst_ref=dst, send_sem=send, recv_sem=recv, device_id=who, device_id_type=MESH
    )


class Gather:
    def __init__(self, own, full, sems, at):
        self.own, self.full, self.sems, self.at = own, full, sems, at
        self.n = own.shape[1]
        self.u = self.n // 12
        r, h = place()
        self.r, self.h = r, h
        y, z = r % 2, (r // 2) % 2
        self.k = 2 * z + y
        self.ky = 2 * z + 1 - y
        self.kz = 2 * (1 - z) + y
        self.kd = 3 - self.k
        self.hx = flip(h, 2)
        self.hc = flip(h, 1)
        self.by_x = (r, self.hx)
        self.by_c = (r, self.hc)
        self.by_y = (flip(r, 1), h)
        self.by_z = (flip(r, 2), h)

    def rows(self, shard, sub, count):
        u = self.u
        return pl.ds(pl.multiple_of(shard * self.n + sub * u, 16), count * u)

    def part(self, slot, who, shard, sub, count, own=False):
        dst = self.full.at[:, self.rows(shard, sub, count), :]
        src = self.own.at[:, self.rows(0, sub, count), :] if own else dst
        send, recv = self.sems
        return remote(src, dst, send.at[self.at, slot], recv.at[self.at, slot], who)

    def x_main(self):
        return self.part(0, self.by_x, self.h, 3 * self.k, 3, own=True)

    def x_diag(self):
        return self.part(1, self.by_x, self.h, 3 * self.kd, 1, own=True)

    def y_main(self):
        return self.part(2, self.by_y, self.hx, 3 * self.k, 3)

    def z_main(self):
        return self.part(3, self.by_z, self.hx, 3 * self.k, 3)

    def y_diag(self):
        return self.part(4, self.by_y, self.hx, 3 * self.kz + 1, 1)

    def z_diag(self):
        return self.part(5, self.by_z, self.hx, 3 * self.ky + 2, 1)

    def c_own(self):
        return self.part(6, self.by_c, self.h, 0, 12, own=True)

    def c_part(self, i):
        return self.part(7 + i, self.by_c, self.hx, 3 * (self.k, self.ky, self.kz, self.kd)[i], 3)

    def local(self):
        send, _ = self.sems
        return pltpu.make_async_copy(
            self.own, self.full.at[:, self.rows(self.h, 0, 12), :], send.at[self.at, 11]
        )

    def start(self):
        self.x_main().start()
        self.x_diag().start()
        self.c_own().start()
        self.local().start()

    def step_x(self):
        self.x_main().wait_recv()
        self.y_main().start()
        self.z_main().start()
        self.c_part(0).start()

    def step_yz(self):
        self.y_main().wait_recv()
        self.z_diag().start()
        self.c_part(1).start()
        self.z_main().wait_recv()
        self.y_diag().start()
        self.c_part(2).start()

    def step_diag(self):
        self.x_diag().wait_recv()
        self.y_diag().wait_recv()
        self.z_diag().wait_recv()
        self.c_part(3).start()

    def near(self):
        self.c_own().wait_recv()
        self.local().wait()

    def far(self):
        for i in range(4):
            self.c_part(i).wait_recv()

    def sent(self):
        for copy in (self.x_main(), self.x_diag(), self.y_main(), self.z_main(), self.y_diag(), self.z_diag(), self.c_own()):
            copy.wait_send()
        for i in range(4):
            self.c_part(i).wait_send()


def window_start(h, j, own_blocks, row_blocks):
    g = own_blocks * h + j
    first = own_blocks * h - HALO
    row = row_blocks * (g // row_blocks)
    return jnp.clip(row, first, first + own_blocks + 2 * HALO - row_blocks) - first


def gather_attend_kernel(
    groups, row_blocks, tok, qkv_own, out_own, up_own, down_own, segk, segq,
    qkv_full, out_full, up_full, down_full, x_win, q_o, k_o, v_o, kt_o, ctx_o, ctxt_o, lse_o, bias,
    xw, w, vt, send, recv, side_send, side_recv, loc,
):
    r, h = place()
    own = tok.shape[0]
    nb = own // BLK
    nw = nb + 2 * HALO
    halo_rows = HALO * BLK
    x_half = (h // 2) % 2
    far_half = 1 - x_half
    half = 2 * qkv_own.shape[1]
    pairs = half // 128

    sems = (send, recv)
    gq = Gather(qkv_own, w, sems, 0)
    go = Gather(out_own, out_full, sems, 1)
    gu = Gather(up_own, up_full, sems, 2)
    gd = Gather(down_own, down_full, sems, 3)

    greet(group_of(r, h, groups) + [gq.by_y, gq.by_z])

    gq.start()
    to_right = remote(tok.at[pl.ds(own - halo_rows, halo_rows), :], xw.at[pl.ds(0, halo_rows), :], side_send.at[0], side_recv.at[0], (r, h + 1))
    to_left = remote(tok.at[pl.ds(0, halo_rows), :], xw.at[pl.ds(halo_rows + own, halo_rows), :], side_send.at[1], side_recv.at[1], (r, h - 1))

    @pl.when(h < groups - 1)
    def _():
        to_right.start()

    @pl.when(h > 0)
    def _():
        to_left.start()

    mine = pltpu.make_async_copy(tok, xw.at[pl.ds(halo_rows, own), :], loc.at[0])
    mine.start()

    @pl.when(h == 0)
    def _():
        xw[pl.ds(0, halo_rows), :] = jnp.zeros((halo_rows, xw.shape[1]), BF)

    @pl.when(h == groups - 1)
    def _():
        xw[pl.ds(halo_rows + own, halo_rows), :] = jnp.zeros((halo_rows, xw.shape[1]), BF)

    for j in range(nb):
        ws = window_start(h, j, nb, row_blocks)
        for kb in range(row_blocks):
            here = segk[pl.ds(pl.multiple_of((ws + kb) * BLK, BLK), BLK), :]
            bias[j, kb] = jnp.where(here == segq[:, j * BLK : (j + 1) * BLK], 0.0, -1e30).astype(F32)

    def project_keys(hx, b):
        base = pl.multiple_of(hx * half, 128)
        xb = xw[pl.ds(pl.multiple_of(b * BLK, BLK), BLK), :]
        wk = w[1, pl.ds(base, half), :]
        wv = w[2, pl.ds(base, half), :]
        key = nt(xb, wk).astype(BF)
        value = nt(xb, wv).astype(BF)
        for i in range(pairs):
            k_o[hx * pairs + i, pl.ds(pl.multiple_of(b * BLK, BLK), BLK), :] = key[:, i * 128 : (i + 1) * 128]
            v_o[hx * pairs + i, pl.ds(pl.multiple_of(b * BLK, BLK), BLK), :] = value[:, i * 128 : (i + 1) * 128]
        kt_o[b, pl.ds(base, half), :] = nt(wk, xb).astype(BF)
        vt[b, pl.ds(base, half), :] = nt(wv, xb).astype(BF)

    def project_query(hx, b):
        base = pl.multiple_of(hx * half, 128)
        xb = xw[pl.ds(pl.multiple_of((b + HALO) * BLK, BLK), BLK), :]
        query = nt(xb, w[0, pl.ds(base, half), :]).astype(BF) * BF(HEAD_WIDTH**-0.5)
        for i in range(pairs):
            q_o[hx * pairs + i, pl.ds(pl.multiple_of(b * BLK, BLK), BLK), :] = query[:, i * 128 : (i + 1) * 128]

    def attend(hx, t):
        j = t // pairs
        p = hx * pairs + t % pairs
        ws = window_start(h, j, nb, row_blocks)
        q = q_o[p, pl.ds(pl.multiple_of(j * BLK, BLK), BLK), :]
        lane = lax.broadcasted_iota(jnp.int32, q.shape, 1)
        for hh in range(2):
            head = 2 * p + hh
            qm = jnp.where(lane // HEAD_WIDTH == hh, q, jnp.zeros_like(q))
            scores = []
            top = None
            for kb in range(row_blocks):
                kblk = k_o[p, pl.ds(pl.multiple_of((ws + kb) * BLK, BLK), BLK), :]
                s = nt(kblk, qm) + bias[j, kb]
                m = jnp.max(s, axis=0, keepdims=True)
                top = m if top is None else jnp.maximum(top, m)
                scores.append(s)
            total = jnp.zeros_like(top)
            acc = jnp.zeros((HEAD_WIDTH, BLK), F32)
            for kb in range(row_blocks):
                e = jnp.exp(scores[kb] - top)
                total = total + jnp.sum(e, axis=0, keepdims=True)
                acc = acc + nn(vt[ws + kb, pl.ds(pl.multiple_of(head * HEAD_WIDTH, HEAD_WIDTH), HEAD_WIDTH), :], e.astype(BF))
            ctxt_o[j, pl.ds(pl.multiple_of(head * HEAD_WIDTH, HEAD_WIDTH), HEAD_WIDTH), :] = acc / total
            lse_o[j, head] = top + jnp.log(total)

    mine.wait()
    gq.near()
    for b in range(nb):
        project_query(x_half, b)
    lax.fori_loop(HALO, HALO + nb, lambda b, c: (project_keys(x_half, b), c)[1], 0)
    gq.step_x()
    go.start()
    gu.start()
    gd.start()

    @pl.when(h > 0)
    def _():
        to_right.wait_recv()

    @pl.when(h < groups - 1)
    def _():
        to_left.wait_recv()

    out_x = pltpu.make_async_copy(xw, x_win, loc.at[1])
    out_x.start()

    def sides(b, c):
        project_keys(x_half, b + jnp.where(b >= HALO, nb, 0))
        return c

    lax.fori_loop(0, 2 * HALO, sides, 0)
    gq.step_yz()
    gq.step_diag()

    steps = nb * pairs

    def first(t, c):
        attend(x_half, t)
        return c

    lax.fori_loop(0, steps, first, 0)
    go.step_x()
    gu.step_x()
    gq.far()
    out_w = pltpu.make_async_copy(w, qkv_full, loc.at[2])
    out_w.start()

    for b in range(nb):
        project_query(far_half, b)
    lax.fori_loop(0, nw, lambda b, c: (project_keys(far_half, b), c)[1], 0)
    go.step_yz()
    gd.step_x()
    go.step_diag()
    gu.step_yz()

    def second(t, c):
        attend(far_half, t)
        return c

    lax.fori_loop(0, steps, second, 0)
    gu.step_diag()
    gd.step_yz()
    gd.step_diag()
    for j in range(nb):
        ctx_o[j * BLK : (j + 1) * BLK, :] = ctxt_o[j].T.astype(BF)
    for g in (go, gu, gd):
        g.near()
        g.far()
    for g in (gq, go, gu, gd):
        g.sent()
    out_x.wait()
    out_w.wait()

    @pl.when(h < groups - 1)
    def _():
        to_right.wait_send()

    @pl.when(h > 0)
    def _():
        to_left.wait_send()


ANY = pl.BlockSpec(memory_space=pl.ANY)
VM = pl.BlockSpec(memory_space=pltpu.VMEM)


def gather_attend(groups, row_blocks, tok, qkv_own, out_own, up_own, down_own, segk, segq):
    own, width = tok.shape
    nb = own // BLK
    nw = nb + 2 * HALO
    all_pairs = groups * qkv_own.shape[1] // 128
    heads = 2 * all_pairs
    s = jax.ShapeDtypeStruct
    full = lambda a: s((a.shape[0], groups * a.shape[1], a.shape[2]), BF)
    outs = [
        (full(qkv_own), ANY),
        (full(out_own), ANY),
        (full(up_own), ANY),
        (full(down_own), ANY),
        (s((nw * BLK, width), BF), ANY),
        (s((all_pairs, own, 128), BF), VM),
        (s((all_pairs, nw * BLK, 128), BF), VM),
        (s((all_pairs, nw * BLK, 128), BF), VM),
        (s((nw, width, BLK), BF), VM),
        (s((own, width), BF), VM),
        (s((nb, width, BLK), F32), VM),
        (s((nb, heads, 1, BLK), F32), VM),
        (s((nb, row_blocks, BLK, BLK), F32), VM),
    ]
    return pl.pallas_call(
        functools.partial(gather_attend_kernel, groups, row_blocks),
        out_shape=[o[0] for o in outs],
        in_specs=[ANY] * 5 + [VM] * 2,
        out_specs=[o[1] for o in outs],
        scratch_shapes=[
            pltpu.VMEM((nw * BLK, width), BF),
            pltpu.VMEM((3, groups * qkv_own.shape[1], width), BF),
            pltpu.VMEM((nw, width, BLK), BF),
            pltpu.SemaphoreType.DMA((4, 12)),
            pltpu.SemaphoreType.DMA((4, 12)),
            pltpu.SemaphoreType.DMA((2,)),
            pltpu.SemaphoreType.DMA((2,)),
            pltpu.SemaphoreType.DMA((3,)),
        ],
        compiler_params=pltpu.CompilerParams(collective_id=0, has_side_effects=True, vmem_limit_bytes=VMEM_LIMIT),
        name="gather_attend",
    )(tok, qkv_own, out_own, up_own, down_own, segk, segq)


def gelu_parts(u):
    bell = jnp.exp(-0.5 * u * u)
    base = 1.0 + (0.3275911 * 0.7071067811865476) * jnp.abs(u)
    t = pl.reciprocal(base, approx=True)
    t = t * (2.0 - base * t)
    poly = t * (0.127414796 + t * (-0.142248368 + t * (0.7107068705 + t * (-0.7265760135 + t * 0.5307027145))))
    tail = poly * bell
    cdf = jnp.where(u >= 0.0, 1.0 - tail, tail)
    return u * cdf, cdf + u * (bell * 0.3989422804014327)


def dense_kernel(
    tok, cot, ctx, ctxt, out_w, up_w, down_w, vec,
    mixed, d_out, d_up, d_down, g_res_o, g_o, gt_delta, vec_o,
    hid, xhat, inv, hl, ht, ffn, act_t, slope, g_low, gup, g_hid,
):
    own, width = tok.shape
    nb = own // BLK
    shards = up_w.shape[0]
    gain1, shift1, gain2, shift2 = (vec[i : i + 1, :].astype(F32) for i in range(4))
    mean = lambda v: jnp.mean(v, axis=1, keepdims=True)
    rows = lambda b: pl.ds(pl.multiple_of(b * BLK, BLK), BLK)
    vec_o[...] = jnp.zeros_like(vec_o)

    def before(b, c):
        resid = tok[rows(b), :].astype(F32) + nn(ctx[rows(b), :], out_w[...])
        cen = resid - mean(resid)
        rs = lax.rsqrt(mean(cen * cen) + NORM_EPS)
        n = cen * rs
        hidden = n * gain1 + shift1
        xhat[rows(b), :] = n
        inv[rows(b), :] = jnp.broadcast_to(rs, (BLK, 128))
        hid[rows(b), :] = hidden
        low = hidden.astype(BF)
        hl[rows(b), :] = low
        ht[b] = low.T
        ffn[rows(b), :] = hidden
        return c

    lax.fori_loop(0, nb, before, 0)

    def forward(t, c):
        s, b = t // nb, t % nb
        up = nn(hl[rows(b), :], up_w[s])
        active, deriv = gelu_parts(up)
        active = active.astype(BF)
        slope[s, rows(b), :] = deriv.astype(BF)
        act_t[s, b] = active.T
        ffn[rows(b), :] += nn(active, down_w[s])
        return c

    lax.fori_loop(0, shards * nb, forward, 0)

    def middle(b, c):
        v = ffn[rows(b), :]
        cen = v - mean(v)
        rs = lax.rsqrt(mean(cen * cen) + NORM_EPS)
        n = cen * rs
        mixed[rows(b), :] = (n * gain2 + shift2).astype(BF)
        ct = cot[rows(b), :].astype(F32)
        vec_o[2:3, :] += jnp.sum(ct * n, axis=0, keepdims=True)
        vec_o[3:4, :] += jnp.sum(ct, axis=0, keepdims=True)
        e = ct * gain2
        g = rs * (e - mean(e) - n * mean(e * n))
        g_hid[rows(b), :] = g
        g_low[rows(b), :] = g.astype(BF)
        return c

    lax.fori_loop(0, nb, middle, 0)

    def backward(s, c):
        def one(b, cc):
            ga = nt(g_low[rows(b), :], down_w[s])
            gu = (slope[s, rows(b), :].astype(F32) * ga).astype(BF)
            gup[rows(b), :] = gu
            g_hid[rows(b), :] += nt(gu, up_w[s])
            return cc

        lax.fori_loop(0, nb, one, 0)

        def grads(i, cc):
            acc_d = jnp.zeros((BLK, width), F32)
            acc_u = jnp.zeros((BLK, width), F32)
            for b in range(nb):
                acc_d += nn(act_t[s, b, rows(i), :], g_low[b * BLK : (b + 1) * BLK, :])
                acc_u += nn(ht[b, rows(i), :], gup[b * BLK : (b + 1) * BLK, :])
            d_down[s, rows(i), :] = acc_d.astype(BF)
            d_up[s, rows(i), :] = acc_u.astype(BF)
            return cc

        lax.fori_loop(0, width // BLK, grads, 0)
        return c

    lax.fori_loop(0, shards, backward, 0)

    def after(b, c):
        g = g_hid[rows(b), :]
        n = xhat[rows(b), :]
        vec_o[0:1, :] += jnp.sum(g * n, axis=0, keepdims=True)
        vec_o[1:2, :] += jnp.sum(g, axis=0, keepdims=True)
        e = g * gain1
        res = inv[rows(b), 0:1] * (e - mean(e) - n * mean(e * n))
        g_res_o[rows(b), :] = res
        low = res.astype(BF)
        g_low[rows(b), :] = low
        gc = nt(low, out_w[...]).astype(BF)
        for i in range(width // 128):
            g_o[i, rows(b), :] = gc[:, i * 128 : (i + 1) * 128]
        gct = nt(out_w[...], low).astype(BF).astype(F32)
        prod = gct * ctxt[b]
        for i in range(width // HEAD_WIDTH):
            gt_delta[b, i] = jnp.sum(prod[i * HEAD_WIDTH : (i + 1) * HEAD_WIDTH, :], axis=0, keepdims=True)
        return c

    lax.fori_loop(0, nb, after, 0)

    def grad_out(i, c):
        acc = jnp.zeros((BLK, width), F32)
        for b in range(nb):
            acc += nn(ctxt[b, rows(i), :].astype(BF), g_low[b * BLK : (b + 1) * BLK, :])
        d_out[rows(i), :] = acc.astype(BF)
        return c

    lax.fori_loop(0, width // BLK, grad_out, 0)


def dense(tok, cot, ctx, ctxt, out_w, up_w, down_w, vec):
    own, width = tok.shape
    nb = own // BLK
    shards = up_w.shape[0]
    heads = width // HEAD_WIDTH
    s = jax.ShapeDtypeStruct
    outs = [
        s((own, width), BF),
        s((width, width), BF),
        s((shards, width, width), BF),
        s((shards, width, width), BF),
        s((own, width), F32),
        s((width // 128, own, 128), BF),
        s((nb, heads, 1, BLK), F32),
        s((8, width), F32),
    ]
    return pl.pallas_call(
        dense_kernel,
        out_shape=outs,
        in_specs=[VM] * 8,
        out_specs=[VM] * len(outs),
        scratch_shapes=[
            pltpu.VMEM((own, width), F32),
            pltpu.VMEM((own, width), F32),
            pltpu.VMEM((own, 128), F32),
            pltpu.VMEM((own, width), BF),
            pltpu.VMEM((nb, width, BLK), BF),
            pltpu.VMEM((own, width), F32),
            pltpu.VMEM((shards, nb, width, BLK), BF),
            pltpu.VMEM((shards, own, width), BF),
            pltpu.VMEM((own, width), BF),
            pltpu.VMEM((own, width), BF),
            pltpu.VMEM((own, width), F32),
        ],
        compiler_params=pltpu.CompilerParams(vmem_limit_bytes=VMEM_LIMIT),
        name="dense",
    )(tok, cot, ctx, ctxt, out_w, up_w, down_w, vec)


def attend_back_kernel(
    groups, row_blocks, q_i, k_i, v_i, kt_i, x_i, g_i, lse, delta, bias, w, g_res,
    d_qkv, gx, gx_left, gx_right,
    dk, dv, dqt, dkt, dvt,
):
    _, h = place()
    all_pairs, own, _ = q_i.shape
    width = x_i.shape[1]
    nb = own // BLK
    nw = nb + 2 * HALO
    rows = lambda b: pl.ds(pl.multiple_of(b * BLK, BLK), BLK)
    dk[...] = jnp.zeros_like(dk)
    dv[...] = jnp.zeros_like(dv)

    def unit(t, c):
        j, p = t // all_pairs, t % all_pairs
        ws = window_start(h, j, nb, row_blocks)
        q = q_i[p, rows(j), :]
        g = g_i[p, rows(j), :]
        lane = lax.broadcasted_iota(jnp.int32, q.shape, 1)
        qm = [jnp.where(lane // HEAD_WIDTH == hh, q, jnp.zeros_like(q)) for hh in range(2)]
        gm = [jnp.where(lane // HEAD_WIDTH == hh, g, jnp.zeros_like(g)) for hh in range(2)]
        acc = [jnp.zeros((HEAD_WIDTH, BLK), F32) for _ in range(2)]
        for kb in range(row_blocks):
            kblk = k_i[p, rows(ws + kb), :]
            vblk = v_i[p, rows(ws + kb), :]
            add_k = None
            for hh in range(2):
                head = 2 * p + hh
                s = nt(kblk, qm[hh]) + bias[j, kb]
                prob = jnp.exp(s - lse[j, head])
                gp = nt(vblk, gm[hh])
                gs = (prob * (gp - delta[j, head])).astype(BF)
                one_v = nn(prob.astype(BF), gm[hh])
                one_k = nn(gs, qm[hh])
                add_k, add_v = (one_k, one_v) if add_k is None else (add_k + one_k, add_v + one_v)
                acc[hh] += nn(kt_i[ws + kb, pl.ds(pl.multiple_of(head * HEAD_WIDTH, HEAD_WIDTH), HEAD_WIDTH), :], gs)
            dk[p, rows(ws + kb), :] += add_k
            dv[p, rows(ws + kb), :] += add_v
        for hh in range(2):
            head = 2 * p + hh
            dqt[j, pl.ds(pl.multiple_of(head * HEAD_WIDTH, HEAD_WIDTH), HEAD_WIDTH), :] = (acc[hh] * HEAD_WIDTH**-0.5).astype(BF)
        return c

    lax.fori_loop(0, nb * all_pairs, unit, 0)

    for b in range(nw):
        lo, hi = b * BLK, (b + 1) * BLK
        kb = jnp.concatenate([dk[p, lo:hi, :].astype(BF) for p in range(all_pairs)], axis=1)
        vb = jnp.concatenate([dv[p, lo:hi, :].astype(BF) for p in range(all_pairs)], axis=1)
        total = nn(kb, w[1]) + nn(vb, w[2])
        dkt[b] = kb.T
        dvt[b] = vb.T
        if HALO <= b < HALO + nb:
            j = b - HALO
            total = total + nn(dqt[j].T, w[0])
            gx[j * BLK : (j + 1) * BLK, :] = g_res[j * BLK : (j + 1) * BLK, :] + total
        elif b < HALO:
            gx_left[lo:hi, :] = total.astype(BF)
        else:
            k = b - HALO - nb
            gx_right[k * BLK : (k + 1) * BLK, :] = total.astype(BF)

    def grads(i, c):
        acc = jnp.zeros((BLK, width), F32)
        for j in range(nb):
            acc += nn(dqt[j, rows(i), :], x_i[(HALO + j) * BLK : (HALO + j + 1) * BLK, :])
        d_qkv[0, rows(i), :] = acc.astype(BF)
        for a, src in ((1, dkt), (2, dvt)):
            acc = jnp.zeros((BLK, width), F32)
            for b in range(nw):
                acc += nn(src[b, rows(i), :], x_i[b * BLK : (b + 1) * BLK, :])
            d_qkv[a, rows(i), :] = acc.astype(BF)
        return c

    lax.fori_loop(0, width // BLK, grads, 0)


def attend_back(groups, row_blocks, q, k, v, kt, x, g, lse, delta, bias, w, g_res):
    all_pairs, own, _ = q.shape
    width = x.shape[1]
    nb = own // BLK
    nw = nb + 2 * HALO
    s = jax.ShapeDtypeStruct
    outs = [
        s((3, width, width), BF),
        s((own, width), F32),
        s((HALO * BLK, width), BF),
        s((HALO * BLK, width), BF),
    ]
    return pl.pallas_call(
        functools.partial(attend_back_kernel, groups, row_blocks),
        out_shape=outs,
        in_specs=[VM] * 11,
        out_specs=[VM] * len(outs),
        scratch_shapes=[
            pltpu.VMEM((all_pairs, nw * BLK, 128), F32),
            pltpu.VMEM((all_pairs, nw * BLK, 128), F32),
            pltpu.VMEM((nb, width, BLK), BF),
            pltpu.VMEM((nw, width, BLK), BF),
            pltpu.VMEM((nw, width, BLK), BF),
        ],
        compiler_params=pltpu.CompilerParams(vmem_limit_bytes=VMEM_LIMIT),
        name="attend_back",
    )(q, k, v, kt, x, g, lse, delta, bias, w, g_res)


class Reduce:
    def __init__(self, src, shard_rows, lo, n, bits, bufs, sems, at):
        self.src, self.N, self.lo, self.n, self.bits = src, shard_rows, lo, n, bits
        self.rc, self.far, self.res, self.rx, self.ry, self.rz, self.rest = bufs
        self.send, self.recv = sems
        self.at = at
        r, h = place()
        self.h = h
        self.y, self.z = r % 2, (r // 2) % 2
        self.hx, self.hc = flip(h, 2), flip(h, 1)
        self.by_x, self.by_c = (r, self.hx), (r, self.hc)
        self.by_y, self.by_z = (flip(r, 1), h), (flip(r, 2), h)
        self.by_rest = [(flip(r, b), h) for b in bits]

    def copy(self, slot, src, dst, who):
        return remote(src, dst, self.send.at[self.at, slot], self.recv.at[self.at, slot], who)

    def shard(self, s):
        return self.src.at[:, pl.ds(pl.multiple_of(s * self.N + self.lo, 16), self.n), :]

    def core(self, i):
        s = flip(self.hc, 2) if i == 0 else self.hc
        return self.copy(i, self.shard(s), self.rc.at[i], self.by_c)

    def start(self):
        self.core(0).start()
        self.core(1).start()

    def x(self):
        return self.copy(2, self.far, self.rx, self.by_x)

    def step_core(self):
        self.core(0).wait_recv()
        self.far[...] = (self.shard(self.hx)[...].astype(F32) + self.rc[0].astype(F32)).astype(BF)
        self.x().start()
        self.core(1).wait_recv()
        self.res[...] = (self.shard(self.h)[...].astype(F32) + self.rc[1].astype(F32)).astype(BF)

    def half(self, which):
        return self.res.at[:, pl.ds(pl.multiple_of(which * (self.n // 2), 16), self.n // 2), :]

    def quarter(self, half, which):
        return self.res.at[:, pl.ds(pl.multiple_of(half * (self.n // 2) + which * (self.n // 4), 16), self.n // 4), :]

    def landed(self, half, which):
        return self.rx.at[:, pl.ds(pl.multiple_of(half * (self.n // 2) + which * (self.n // 4), 16), self.n // 4), :]

    def y_down(self):
        return self.copy(3, self.half(1 - self.y), self.ry, self.by_y)

    def z_down(self):
        return self.copy(4, self.quarter(self.y, 1 - self.z), self.rz, self.by_z)

    def z_up(self):
        return self.copy(5, self.quarter(self.y, self.z), self.landed(self.y, self.z), self.by_z)

    def y_up(self):
        return self.copy(6, self.quarter(self.y, self.z), self.landed(self.y, self.z), self.by_y)

    def y_up2(self):
        return self.copy(7, self.landed(self.y, 1 - self.z), self.landed(self.y, 1 - self.z), self.by_y)

    def swap(self, i):
        return self.copy(8 + i, self.quarter(self.y, self.z), self.rest.at[i], self.by_rest[i])

    def add(self, ref, got):
        ref[...] = (ref[...].astype(F32) + got[...].astype(F32)).astype(BF)

    def step_x(self):
        self.x().wait_recv()
        self.add(self.res, self.rx)
        self.y_down().start()

    def step_y(self):
        self.y_down().wait_recv()
        self.add(self.half(self.y), self.ry)
        self.z_down().start()

    def step_z(self):
        self.z_down().wait_recv()
        self.add(self.quarter(self.y, self.z), self.rz)
        if self.bits:
            self.swap(0).start()

    def step_rest(self, i):
        self.swap(i).wait_recv()
        self.swap(i).wait_send()
        self.add(self.quarter(self.y, self.z), self.rest.at[i])
        if i + 1 < len(self.bits):
            self.swap(i + 1).start()

    def step_up(self):
        self.z_up().start()
        self.y_up().start()

    def step_up2(self):
        self.z_up().wait_recv()
        self.y_up2().start()

    def step_end(self):
        self.y_up().wait_recv()
        self.y_up2().wait_recv()

    def store(self, out):
        q = self.n // 4
        for half in range(2):
            for which in range(2):
                lo = half * (self.n // 2) + which * q
                mine = jnp.logical_and(self.y == half, self.z == which)
                for there, src in ((mine, self.res), (jnp.logical_not(mine), self.rx)):

                    @pl.when(there)
                    def _():
                        out[:, self.lo + lo : self.lo + lo + q, :] = src[:, lo : lo + q, :].astype(F32)

    def steps(self):
        return (
            [self.start, self.step_core, self.step_x, self.step_y, self.step_z]
            + [functools.partial(self.step_rest, i) for i in range(len(self.bits))]
            + [self.step_up, self.step_up2, self.step_end]
        )

    def sent(self):
        for c in (self.core(0), self.core(1), self.x(), self.y_down(), self.z_down(), self.z_up(), self.y_up(), self.y_up2()):
            c.wait_send()


def other_bits(count):
    bits, b = [], 4
    while b < count:
        bits.append(b)
        b *= 2
    return tuple(bits)


def chunk_plan(width, shard_qkv):
    plan = []
    for a in (0, 1):
        for lo in range(0, width, width // 2):
            plan.append((a, 1, width, lo, width // 2))
    plan.append((2, 1, shard_qkv, 0, shard_qkv))
    plan.append((3, 3, shard_qkv, 0, shard_qkv))
    return plan


def reduce_kernel(
    groups, plan, bits, d_down, d_up, d_out, d_qkv, gx, gx_left, gx_right, vec,
    o_down, o_up, o_out, o_qkv, o_tok, o_vec,
    *scratch,
):
    r, h = place()
    n = len(plan)
    bufs = [scratch[i * 7 : (i + 1) * 7] for i in range(n)]
    send, recv, side_send, side_recv, vsend, vrecv, side, vin, vacc = scratch[7 * n :]
    srcs = (d_down, d_up, d_out, d_qkv)
    dsts = (o_down, o_up, o_out, o_qkv)
    parts = [Reduce(srcs[a], rows, lo, cnt, bits, bufs[i], (send, recv), i) for i, (a, m, rows, lo, cnt) in enumerate(plan)]
    one = parts[0]
    greet(group_of(r, h, groups) + [one.by_y, one.by_z] + one.by_rest)

    halo = gx_left.shape[0]
    own = gx.shape[0]
    to_left = remote(gx_left, side.at[1], side_send.at[0], side_recv.at[0], (r, h - 1))
    to_right = remote(gx_right, side.at[0], side_send.at[1], side_recv.at[1], (r, h + 1))

    @pl.when(h > 0)
    def _():
        to_left.start()

    @pl.when(h < groups - 1)
    def _():
        to_right.start()

    vec_ids = [one.by_c, one.by_x, one.by_y, one.by_z] + one.by_rest

    def vstep(i):
        src = vec if i == 0 else vacc.at[i - 1]
        return remote(src, vin.at[i], vsend.at[i], vrecv.at[i], vec_ids[i])

    vstep(0).start()

    def vnext(i):
        vstep(i).wait_recv()
        before = vec[...] if i == 0 else vacc[i - 1]
        vacc[i] = before + vin[i]
        if i + 1 < len(vec_ids):
            vstep(i + 1).start()

    lists = [p.steps() for p in parts]
    depth = len(lists[0])
    tick = 0
    for tick in range(n + depth - 1):
        for i in range(n):
            s = tick - i
            if 0 <= s < depth:
                lists[i][s]()
                if s == depth - 1:
                    a, m, rows, lo, cnt = plan[i]
                    parts[i].store(dsts[a])
        if tick < len(vec_ids):
            vnext(tick)
    for i in range(n + depth - 1, len(vec_ids)):
        vnext(i)
    o_vec[...] = vacc[len(vec_ids) - 1]

    o_tok[...] = gx[...]

    @pl.when(h < groups - 1)
    def _():
        to_left.wait_recv()
        o_tok[own - halo :, :] += side[1].astype(F32)

    @pl.when(h > 0)
    def _():
        to_right.wait_recv()
        o_tok[:halo, :] += side[0].astype(F32)

    for p in parts:
        p.sent()
    for i in range(len(vec_ids)):
        vstep(i).wait_send()

    @pl.when(h > 0)
    def _():
        to_left.wait_send()

    @pl.when(h < groups - 1)
    def _():
        to_right.wait_send()


def reduce(groups, row_devices, d_down, d_up, d_out, d_qkv, gx, gx_left, gx_right, vec):
    width = gx.shape[1]
    s_qkv = d_qkv.shape[1] // groups
    plan = chunk_plan(width, s_qkv)
    bits = other_bits(row_devices)
    scratch = []
    for a, m, rows, lo, cnt in plan:
        scratch += [
            pltpu.VMEM((2, m, cnt, width), BF),
            pltpu.VMEM((m, cnt, width), BF),
            pltpu.VMEM((m, cnt, width), BF),
            pltpu.VMEM((m, cnt, width), BF),
            pltpu.VMEM((m, cnt // 2, width), BF),
            pltpu.VMEM((m, cnt // 4, width), BF),
            pltpu.VMEM((max(1, len(bits)), m, cnt // 4, width), BF),
        ]
    hops = 4 + len(bits)
    scratch += [
        pltpu.SemaphoreType.DMA((len(plan), 8 + len(bits))),
        pltpu.SemaphoreType.DMA((len(plan), 8 + len(bits))),
        pltpu.SemaphoreType.DMA((2,)),
        pltpu.SemaphoreType.DMA((2,)),
        pltpu.SemaphoreType.DMA((hops,)),
        pltpu.SemaphoreType.DMA((hops,)),
        pltpu.VMEM((2,) + gx_left.shape, BF),
        pltpu.VMEM((hops,) + vec.shape, F32),
        pltpu.VMEM((hops,) + vec.shape, F32),
    ]
    s = jax.ShapeDtypeStruct
    outs = [
        s((1, width, width), F32),
        s((1, width, width), F32),
        s((1, s_qkv, width), F32),
        s((3, s_qkv, width), F32),
        s(gx.shape, F32),
        s(vec.shape, F32),
    ]
    return pl.pallas_call(
        functools.partial(reduce_kernel, groups, plan, bits),
        out_shape=outs,
        in_specs=[VM] * 8,
        out_specs=[VM] * len(outs),
        scratch_shapes=scratch,
        compiler_params=pltpu.CompilerParams(collective_id=1, has_side_effects=True, vmem_limit_bytes=VMEM_LIMIT),
        name="reduce",
    )(d_down, d_up, d_out, d_qkv, gx, gx_left, gx_right, vec)


def local(
    groups, row_devices,
    tokens, lengths, w_query, w_key, w_value, w_out, w_up, w_down,
    gain_first, shift_first, gain_second, shift_second, cotangent,
):
    packed_rows = lengths.shape[0]
    own, width = tokens.shape
    row_length = groups * own // packed_rows
    row_blocks = row_length // BLK
    nw = own // BLK + 2 * HALO
    h = lax.axis_index("heads")

    vec = lax.all_gather(jnp.stack([gain_first, shift_first, gain_second, shift_second]), "heads", axis=1, tiled=True)
    doc_ends = jnp.cumsum(lengths, axis=1)
    position = lax.broadcasted_iota(jnp.int32, (packed_rows, row_length, lengths.shape[1]), 1)
    span = jnp.sum((position >= doc_ends[:, None, :]).astype(jnp.int32), axis=2)
    ids = span + lengths.shape[1] * lax.broadcasted_iota(jnp.int32, span.shape, 0)
    ids = jnp.pad(ids.reshape(-1), (HALO * BLK, HALO * BLK), constant_values=-1)
    seg_k = lax.dynamic_slice(ids, (own * h,), (nw * BLK,))
    seg_q = seg_k[HALO * BLK : HALO * BLK + own]

    qkv_own = jnp.stack([w_query.T, w_key.T, w_value.T])
    shard_cols = w_up.shape[1]
    (qkv, out_w, up_w, down_w, x_win, q, k, v, kt, ctx, ctxt, lse, bias) = gather_attend(
        groups, row_blocks, tokens, qkv_own, w_out[None], w_up[None], w_down[None], seg_k[:, None], seg_q[None, :]
    )
    up_w = up_w.reshape(groups, width, shard_cols)
    down_w = down_w.reshape(groups, shard_cols, width)
    mixed, d_out, d_up, d_down, g_res, g, delta, vec_grads = dense(tokens, cotangent, ctx, ctxt, out_w[0], up_w, down_w, vec)
    d_qkv, gx, gx_left, gx_right = attend_back(groups, row_blocks, q, k, v, kt, x_win, g, lse, delta, bias, qkv, g_res)
    o_down, o_up, o_out, o_qkv, o_tok, o_vec = reduce(
        groups, row_devices,
        d_down.reshape(1, -1, width), d_up.reshape(1, -1, width), d_out[None], d_qkv, gx, gx_left, gx_right, vec_grads,
    )
    n = gain_first.shape[0]
    mine = lax.dynamic_slice(o_vec, (0, n * h), (4, n))
    return (
        mixed, o_tok, o_qkv[0].T, o_qkv[1].T, o_qkv[2].T, o_out[0], o_up[0], o_down[0],
        mine[0], mine[1], mine[2], mine[3],
    )


def solution(mesh):
    both, heads = P(("rows", "heads"), None), P("heads")
    cols, rows = P(None, "heads"), P("heads", None)
    return jax.shard_map(
        functools.partial(local, mesh.shape["heads"], mesh.shape["rows"]),
        mesh=mesh,
        in_specs=(both, P("rows", None), cols, cols, cols, rows, cols, rows, heads, heads, heads, heads, both),
        out_specs=(both, both, cols, cols, cols, rows, cols, rows, heads, heads, heads, heads),
        check_vma=False,
    )
```

time: 773 us -> 389 us (0.50); the launches traced: 763 us -> 389 us
  Pallas kernels: 0 us -> 365 us
  waiting for transfers between devices: 359 us -> 0 us
  matrix products: 215 us -> 0 us
  blocking collectives: 67.4 us -> 5.35 us
  other arithmetic: 45.8 us -> 3.24 us
  local copies, waits for them, and re-layouts: 53.7 us -> 13.9 us
  between operations: 16.1 us -> 0.78 us
    pallas_call x0 -> x4, Pallas kernels: none -> 365 us  [the longest x1 147 us: reduce(): pl.pallas_call(functools.partial(reduce_kernel, groups, plan, bits), out_...]
    psum x1 -> x0, waiting for transfers between devices: 237 us -> none  [local(): lax.psum((grad_query, grad_key, grad_value, part_out, part_up, part_down,...]
    dot_general x39 -> x0, matrix products: 215 us -> none  [the longest x6 37.2 us: contract_first(): lax.dot_general(left, right, (((0,), (0,)), ((), ())), preferred_element_...]
    reduce_scatter x4 -> x0, waiting for transfers between devices: 78.8 us -> none  [the longest x1 45.4 us: local(): lax.psum_scatter(term_sum, 'heads', scatter_dimension=0, tiled=True)]
    all_gather x4 -> x0, waiting for transfers between devices: 40.1 us -> none  [the longest x1 40 us: local(): group_tok = lax.all_gather(tokens, 'heads', axis=0, tiled=True)]
    unnamed x2 -> x0, blocking collectives: 25.6 us -> none
    psum x1 -> x0, blocking collectives: 22 us -> none  [local(): lax.psum((grad_query, grad_key, grad_value, part_out, part_up, part_down,...]
    convert_element_type x7 -> x0, other arithmetic: 21.1 us -> none  [the longest x3 21.1 us: backward_row(): grad_scores = (attn_probs * (grad_probs - row_delta)).astype(bf16)]
  transfers between devices with their start and end apart: 10 -> 0, of which waited for: 4 -> 0; matrix products, arithmetic and copies ran while one was open for 34% -> 0% of each run, Pallas kernels for 0% -> 0%
where the time goes in v1:
time: 389 us
  Pallas kernels  365 us (94%)
  local copies, waits for them, and re-layouts  13.9 us (4%)
  blocking collectives  5.35 us (1%)
    pallas_call x1, Pallas kernels, reduce(): pl.pallas_call(functools.partial(reduce_kernel, groups, plan, bits), out_...  147 us
    pallas_call x1, Pallas kernels, gather_attend(): pl.pallas_call(functools.partial(gather_attend_kernel, groups, row_blocks...  100 us
    pallas_call x1, Pallas kernels, attend_back(): pl.pallas_call(functools.partial(attend_back_kernel, groups, row_blocks),...  59.9 us
    pallas_call x1, Pallas kernels, dense(): pl.pallas_call(dense_kernel, out_shape=outs, in_specs=[VM] * 8, out_specs...  58.2 us

profile of v1, /device:TPU:0, one launch (start us, length us, event | category | flops | bytes accessed | tf_op | source)
XLA Modules:
  0.0 388.7 jit_solution(5529772974785528224)
XLA Ops:
  0.6 0.9 reduce_window_sum.11
  1.5 0.1 convert_reduce_fusion
  1.7 0.1 broadcast_add_fusion
  1.8 0.1 pad_dynamic-slice_fusion.1
  1.8 1.2 broadcast_in_dim.25.segk
  3.1 0.1 pad_dynamic-slice_fusion
  3.1 0.6 broadcast_in_dim.23.segq
  3.7 2.1 pad_maximum_fusion.qkv_own
  5.9 0.0 copy-start.4
  5.9 0.0 copy-start.5
  5.9 100.0 %gather_attend.1 = (bf16[3,768,768]{2,1,0:T(8,128)(2,1)}, bf16[1,768,768]{2,1,0:T(8,128)(2,1)}, bf16[1,3072,768]{2,1,0:T(8,128)(2,1)}, bf16[1,3072,768]{2,1,0:T(...) custom-call(bf16[768,768]{1,0:T(8,128)(2,1)} %tok.3, ...), custom_call_target="tpu_custom_call" | custom-call | tf_op jit(solution)/shard_map/gather_attend/pallas_call | solution.py:364
  105.9 0.0 copy-done.4
  105.9 0.0 copy-done.5
  105.9 0.0 copy-done.6
  105.9 0.0 copy-done.7
  106.0 5.3 %all-gather = bf16[4,192,4]{1,2,0:T(4,128)(2,1)S(1)} all-gather(bf16[1,192,4]{1,2,0:T(4,128)(2,1)S(1)} %maximum_bitcast_fusion), channel_id=1, replica_groups=mesh['rows'=8,'heads'=4] {'heads'}, dimensions={0}, use_global_device_ids=true | all-gather | bytes 7680 | tf_op jit(solution)/shard_map/all_gather | solution.py:947
  111.3 0.7 reshape.48
  112.0 58.2 %dense.1 = (bf16[768,768]{1,0:T(8,128)(2,1)}, bf16[768,768]{1,0:T(8,128)(2,1)}, bf16[4,768,768]{2,1,0:T(8,128)(2,1)}, bf16[4,768,768]{2,1,0:T(8,128)(2,1)}, f32[...) custom-call(bf16[768,768]{1,0:T(8,128)(2,1)} %tok.3, ...), custom_call_target="tpu_custom_call" | custom-call | tf_op jit(solution)/shard_map/dense/pallas_call | solution.py:526
  170.2 59.9 %attend_back.1 = (bf16[3,768,768]{2,1,0:T(8,128)(2,1)}, f32[768,768]{1,0:T(8,128)}, bf16[512,768]{1,0:T(8,128)(2,1)}, bf16[512,768]{1,0:T(8,128)(2,1)}) custom-call(bf16[6,768,128]{2,1,0:T(8,128)(2,1)} %get-tuple-element.52.q_i, bf16[6,1792,128]{2,1,0:T(8,128)(2,1)} %get-tuple-element.53.k_i, bf16[6,1792,128]{2,1,0:T(8,128)(2,1)} %get-tuple-element.54.v_i, ...), custom_call_target="tpu_custom_call" | custom-call | tf_op jit(solution)/shard_map/attend_back/pallas_call | solution.py:639
  230.1 147.4 %reduce.1 = (f32[1,768,768]{2,1,0:T(8,128)}, f32[1,768,768]{2,1,0:T(8,128)}, f32[1,192,768]{2,1,0:T(8,128)}, f32[3,192,768]{2,1,0:T(8,128)}, f32[768,768]{1,0:T(8,128)}, /*index=5*/f32[8,768]{1,0:T(8,128)}) custom-call(bf16[1,3072,768]{2,1,0:T(8,128)(2,1)} %bitcast.47, bf16[1,3072,768]{2,1,0:T(8,128)(2,1)} %bitcast.46, bf16[1,768,768]{2,1,0:T(8,128)(2,1)} %bitcast.51, ...), custom_call_target="tpu_custom_call" | custom-call | tf_op jit(solution)/shard_map/reduce/pallas_call | solution.py:924
  377.5 0.0 copy-start.2
  377.5 2.8 slice_bitcast_fusion
  380.3 1.5 fusion
  381.8 0.0 copy-done.2
  381.8 0.0 copy-start.1
  381.8 1.4 copy.35
  383.3 0.0 copy-done.3
  383.3 0.8 copy.36
  384.1 0.7 copy-done.1
  384.8 1.4 copy.37
  386.2 1.1 copy-done
  387.3 1.4 copy.38
  (12 shorter events, 0.1 us)
Async XLA Ops:
  5.9 100.0 %copy-start.4 = (bf16[192]{0:T(256)(128)(2,1)S(1)}, bf16[192]{0:T(256)(128)(2,1)}, u32[]{:S(2)}) copy-start(bf16[192]{0:T(256)(128)(2,1)} %param.21) | copy-start | bytes 1156
  5.9 100.0 %copy-start.5 = (bf16[192]{0:T(256)(128)(2,1)S(1)}, bf16[192]{0:T(256)(128)(2,1)}, u32[]{:S(2)}) copy-start(bf16[192]{0:T(256)(128)(2,1)} %param.22) | copy-start | bytes 1156
  5.9 100.0 %copy-start.6 = (bf16[192]{0:T(256)(128)(2,1)S(1)}, bf16[192]{0:T(256)(128)(2,1)}, u32[]{:S(2)}) copy-start(bf16[192]{0:T(256)(128)(2,1)} %param.23) | copy-start | bytes 1156
  5.9 100.1 %copy-start.7 = (bf16[192]{0:T(256)(128)(2,1)S(1)}, bf16[192]{0:T(256)(128)(2,1)}, u32[]{:S(2)}) copy-start(bf16[192]{0:T(256)(128)(2,1)} %param.24) | copy-start | bytes 1156
  377.5 4.3 %copy-start.2 = (f32[768,768]{1,0:T(8,128)S(1)}, f32[768,768]{1,0:T(8,128)}, u32[]{:S(2)}) copy-start(f32[768,768]{1,0:T(8,128)} %get-tuple-element.94) | copy-start | bytes 7077892
  381.8 1.4 copy-start.3
  381.8 2.9 copy-start.1
  384.8 2.5 copy-start

commit v2 on v1

v2 whole, which is shorter than its diff:
```python
import functools

import jax
import jax.numpy as jnp
from jax import lax
from jax.experimental import pallas as pl
from jax.experimental.pallas import tpu as pltpu
from jax.sharding import PartitionSpec as P

MESH = pl.DeviceIdType.MESH
BF = jnp.bfloat16
F32 = jnp.float32
HEAD_WIDTH = 64
LONGEST_DOC = 512
BLK = 256
HALO = LONGEST_DOC // BLK
NORM_EPS = 1e-12
VMEM_LIMIT = 62 * 1024 * 1024


def nt(left, right):
    return lax.dot_general(left, right, (((1,), (1,)), ((), ())), preferred_element_type=F32)


def nn(left, right):
    return lax.dot_general(left, right, (((1,), (0,)), ((), ())), preferred_element_type=F32)


def flip(index, bit):
    return index + bit - 2 * bit * ((index // bit) % 2)


def place():
    r, h = lax.axis_index("rows"), lax.axis_index("heads")
    return r, h


def greet(ids):
    barrier = pltpu.get_barrier_semaphore()
    for who in ids:
        pl.semaphore_signal(barrier, inc=1, device_id=who, device_id_type=MESH)
    pl.semaphore_wait(barrier, len(ids))


def group_of(r, h, groups):
    return [(r, lax.rem(h + i, groups)) for i in range(1, groups)]


def remote(src, dst, send, recv, who):
    return pltpu.make_async_remote_copy(
        src_ref=src, dst_ref=dst, send_sem=send, recv_sem=recv, device_id=who, device_id_type=MESH
    )


class Gather:
    def __init__(self, own, full, sems, at):
        self.own, self.full, self.sems, self.at = own, full, sems, at
        self.n = own.shape[1]
        self.u = self.n // 12
        r, h = place()
        self.r, self.h = r, h
        y, z = r % 2, (r // 2) % 2
        self.k = 2 * z + y
        self.ky = 2 * z + 1 - y
        self.kz = 2 * (1 - z) + y
        self.kd = 3 - self.k
        self.hx = flip(h, 2)
        self.hc = flip(h, 1)
        self.by_x = (r, self.hx)
        self.by_c = (r, self.hc)
        self.by_y = (flip(r, 1), h)
        self.by_z = (flip(r, 2), h)

    def rows(self, shard, sub, count):
        u = self.u
        return pl.ds(pl.multiple_of(shard * self.n + sub * u, 16), count * u)

    def part(self, slot, who, shard, sub, count, own=False):
        dst = self.full.at[:, self.rows(shard, sub, count), :]
        src = self.own.at[:, self.rows(0, sub, count), :] if own else dst
        send, recv = self.sems
        return remote(src, dst, send.at[self.at, slot], recv.at[self.at, slot], who)

    def x_main(self):
        return self.part(0, self.by_x, self.h, 3 * self.k, 3, own=True)

    def x_diag(self):
        return self.part(1, self.by_x, self.h, 3 * self.kd, 1, own=True)

    def y_main(self):
        return self.part(2, self.by_y, self.hx, 3 * self.k, 3)

    def z_main(self):
        return self.part(3, self.by_z, self.hx, 3 * self.k, 3)

    def y_diag(self):
        return self.part(4, self.by_y, self.hx, 3 * self.kz + 1, 1)

    def z_diag(self):
        return self.part(5, self.by_z, self.hx, 3 * self.ky + 2, 1)

    def c_own(self):
        return self.part(6, self.by_c, self.h, 0, 12, own=True)

    def c_part(self, i):
        return self.part(7 + i, self.by_c, self.hx, 3 * (self.k, self.ky, self.kz, self.kd)[i], 3)

    def local(self):
        send, _ = self.sems
        return pltpu.make_async_copy(
            self.own, self.full.at[:, self.rows(self.h, 0, 12), :], send.at[self.at, 11]
        )

    def start_x(self):
        self.x_main().start()
        self.x_diag().start()

    def start_c(self):
        self.c_own().start()
        self.local().start()

    def step_x(self):
        self.x_main().wait_recv()
        self.y_main().start()
        self.z_main().start()
        self.c_part(0).start()

    def step_yz(self):
        self.y_main().wait_recv()
        self.z_diag().start()
        self.c_part(1).start()
        self.z_main().wait_recv()
        self.y_diag().start()
        self.c_part(2).start()

    def step_diag(self):
        self.x_diag().wait_recv()
        self.y_diag().wait_recv()
        self.z_diag().wait_recv()
        self.c_part(3).start()

    def near(self):
        self.c_own().wait_recv()
        self.local().wait()

    def far(self):
        for i in range(4):
            self.c_part(i).wait_recv()

    def sent(self):
        for copy in (self.x_main(), self.x_diag(), self.y_main(), self.z_main(), self.y_diag(), self.z_diag(), self.c_own()):
            copy.wait_send()
        for i in range(4):
            self.c_part(i).wait_send()


def window_start(h, j, own_blocks, row_blocks):
    g = own_blocks * h + j
    first = own_blocks * h - HALO
    row = row_blocks * (g // row_blocks)
    return jnp.clip(row, first, first + own_blocks + 2 * HALO - row_blocks) - first


def mask_of(keys, queries):
    down = jnp.broadcast_to(keys, (8, BLK)).T[:, 0:1]
    return jnp.where(down == queries, 0.0, -1e30).astype(F32)


def gather_attend_kernel(
    groups, row_blocks, tok, qkv_own, out_own, up_own, down_own, vec_own, seg,
    qkv_full, out_full, up_full, down_full, vec_all, x_win, q_o, k_o, v_o, kt_o, ctx_o, ctxt_o, lse_o,
    bias, xw, w, vt, send, recv, side_send, side_recv, vec_send, vec_recv, loc,
):
    r, h = place()
    own = tok.shape[0]
    nb = own // BLK
    nw = nb + 2 * HALO
    halo_rows = HALO * BLK
    x_half = (h // 2) % 2
    far_half = 1 - x_half
    half = 2 * qkv_own.shape[1]
    pairs = half // 128

    sems = (send, recv)
    gq = Gather(qkv_own, w, sems, 0)
    go = Gather(out_own, out_full, sems, 1)
    gu = Gather(up_own, up_full, sems, 2)
    gd = Gather(down_own, down_full, sems, 3)

    greet(group_of(r, h, groups) + [gq.by_y, gq.by_z])

    gq.start_c()
    to_right = remote(tok.at[pl.ds(own - halo_rows, halo_rows), :], xw.at[pl.ds(0, halo_rows), :], side_send.at[0], side_recv.at[0], (r, h + 1))
    to_left = remote(tok.at[pl.ds(0, halo_rows), :], xw.at[pl.ds(halo_rows + own, halo_rows), :], side_send.at[1], side_recv.at[1], (r, h - 1))

    @pl.when(h < groups - 1)
    def _():
        to_right.start()

    @pl.when(h > 0)
    def _():
        to_left.start()

    gq.start_x()
    mine = pltpu.make_async_copy(tok, xw.at[pl.ds(halo_rows, own), :], loc.at[0])
    mine.start()

    def vec_to(i):
        who = (r, lax.rem(h + 1 + i, groups))
        return remote(vec_own, vec_all.at[h], vec_send.at[i], vec_recv.at[groups - 2 - i], who)

    def vec_from(i):
        return remote(vec_own, vec_all.at[h], vec_send.at[i], vec_recv.at[i], (r, lax.rem(h + 1 + i, groups)))

    for i in range(groups - 1):
        vec_to(i).start()
    vec_mine = pltpu.make_async_copy(vec_own, vec_all.at[h], loc.at[3])
    vec_mine.start()

    @pl.when(h == 0)
    def _():
        xw[pl.ds(0, halo_rows), :] = jnp.zeros((halo_rows, xw.shape[1]), BF)

    @pl.when(h == groups - 1)
    def _():
        xw[pl.ds(halo_rows + own, halo_rows), :] = jnp.zeros((halo_rows, xw.shape[1]), BF)

    for j in range(nb):
        ws = window_start(h, j, nb, row_blocks)
        for kb in range(row_blocks):
            bias[j, kb] = mask_of(seg[ws + kb], seg[HALO + j])

    def project_keys(hx, b):
        base = pl.multiple_of(hx * half, 128)
        xb = xw[pl.ds(pl.multiple_of(b * BLK, BLK), BLK), :]
        wk = w[1, pl.ds(base, half), :]
        wv = w[2, pl.ds(base, half), :]
        key = nt(xb, wk).astype(BF)
        value = nt(xb, wv).astype(BF)
        for i in range(pairs):
            k_o[hx * pairs + i, pl.ds(pl.multiple_of(b * BLK, BLK), BLK), :] = key[:, i * 128 : (i + 1) * 128]
            v_o[hx * pairs + i, pl.ds(pl.multiple_of(b * BLK, BLK), BLK), :] = value[:, i * 128 : (i + 1) * 128]
        kt_o[b, pl.ds(base, half), :] = nt(wk, xb).astype(BF)
        vt[b, pl.ds(base, half), :] = nt(wv, xb).astype(BF)

    def project_query(hx, b):
        base = pl.multiple_of(hx * half, 128)
        xb = xw[pl.ds(pl.multiple_of((b + HALO) * BLK, BLK), BLK), :]
        query = nt(xb, w[0, pl.ds(base, half), :]).astype(BF) * BF(HEAD_WIDTH**-0.5)
        for i in range(pairs):
            q_o[hx * pairs + i, pl.ds(pl.multiple_of(b * BLK, BLK), BLK), :] = query[:, i * 128 : (i + 1) * 128]

    def attend(hx, t):
        j = t // pairs
        p = hx * pairs + t % pairs
        ws = window_start(h, j, nb, row_blocks)
        q = q_o[p, pl.ds(pl.multiple_of(j * BLK, BLK), BLK), :]
        lane = lax.broadcasted_iota(jnp.int32, q.shape, 1)
        for hh in range(2):
            head = 2 * p + hh
            qm = jnp.where(lane // HEAD_WIDTH == hh, q, jnp.zeros_like(q))
            scores = []
            top = None
            for kb in range(row_blocks):
                kblk = k_o[p, pl.ds(pl.multiple_of((ws + kb) * BLK, BLK), BLK), :]
                s = nt(kblk, qm) + bias[j, kb]
                m = jnp.max(s, axis=0, keepdims=True)
                top = m if top is None else jnp.maximum(top, m)
                scores.append(s)
            total = jnp.zeros_like(top)
            acc = jnp.zeros((HEAD_WIDTH, BLK), F32)
            for kb in range(row_blocks):
                e = jnp.exp(scores[kb] - top)
                total = total + jnp.sum(e, axis=0, keepdims=True)
                acc = acc + nn(vt[ws + kb, pl.ds(pl.multiple_of(head * HEAD_WIDTH, HEAD_WIDTH), HEAD_WIDTH), :], e.astype(BF))
            ctxt_o[j, pl.ds(pl.multiple_of(head * HEAD_WIDTH, HEAD_WIDTH), HEAD_WIDTH), :] = acc / total
            lse_o[j, head] = top + jnp.log(total)

    mine.wait()
    gq.near()
    for b in range(nb):
        project_query(x_half, b)
    lax.fori_loop(HALO, HALO + nb, lambda b, c: (project_keys(x_half, b), c)[1], 0)
    gq.step_x()
    go.start_x()
    gu.start_x()
    for g in (go, gu, gd):
        g.start_c()

    @pl.when(h > 0)
    def _():
        to_right.wait_recv()

    @pl.when(h < groups - 1)
    def _():
        to_left.wait_recv()

    out_x = pltpu.make_async_copy(xw, x_win, loc.at[1])
    out_x.start()

    def sides(b, c):
        project_keys(x_half, b + jnp.where(b >= HALO, nb, 0))
        return c

    lax.fori_loop(0, 2 * HALO, sides, 0)

    def attend_all(hx, hooks):
        def body(t, c):
            for at, steps in hooks.items():

                @pl.when(t == at)
                def _():
                    for step in steps:
                        step()

            attend(hx, t)
            return c

        lax.fori_loop(0, nb * pairs, body, 0)

    attend_all(x_half, {0: [gq.step_yz], 1: [gq.step_diag], 2: [go.step_x], 4: [gu.step_x, gd.start_x], 6: [go.step_yz], 7: [go.step_diag]})
    gq.far()
    out_w = pltpu.make_async_copy(w, qkv_full, loc.at[2])
    out_w.start()
    gu.step_yz()

    for b in range(nb):
        project_query(far_half, b)
    lax.fori_loop(0, nw, lambda b, c: (project_keys(far_half, b), c)[1], 0)

    attend_all(far_half, {0: [gu.step_diag, gd.step_x], 4: [gd.step_yz], 6: [gd.step_diag]})
    for j in range(nb):
        ctx_o[j * BLK : (j + 1) * BLK, :] = ctxt_o[j].T.astype(BF)
    for g in (go, gu, gd):
        g.near()
        g.far()
    for g in (gq, go, gu, gd):
        g.sent()
    for i in range(groups - 1):
        vec_to(i).wait_send()
        vec_from(i).wait_recv()
    vec_mine.wait()
    out_x.wait()
    out_w.wait()

    @pl.when(h < groups - 1)
    def _():
        to_right.wait_send()

    @pl.when(h > 0)
    def _():
        to_left.wait_send()


ANY = pl.BlockSpec(memory_space=pl.ANY)
VM = pl.BlockSpec(memory_space=pltpu.VMEM)


def gather_attend(groups, row_blocks, tok, qkv_own, out_own, up_own, down_own, vec_own, seg):
    own, width = tok.shape
    nb = own // BLK
    nw = nb + 2 * HALO
    all_pairs = groups * qkv_own.shape[1] // 128
    heads = 2 * all_pairs
    s = jax.ShapeDtypeStruct
    full = lambda a: s((a.shape[0], groups * a.shape[1], a.shape[2]), BF)
    outs = [
        (full(qkv_own), ANY),
        (full(out_own), ANY),
        (full(up_own), ANY),
        (full(down_own), ANY),
        (s((groups,) + vec_own.shape, BF), ANY),
        (s((nw * BLK, width), BF), ANY),
        (s((all_pairs, own, 128), BF), VM),
        (s((all_pairs, nw * BLK, 128), BF), VM),
        (s((all_pairs, nw * BLK, 128), BF), VM),
        (s((nw, width, BLK), BF), VM),
        (s((own, width), BF), VM),
        (s((nb, width, BLK), F32), VM),
        (s((nb, heads, 1, BLK), F32), VM),
    ]
    return pl.pallas_call(
        functools.partial(gather_attend_kernel, groups, row_blocks),
        out_shape=[o[0] for o in outs],
        in_specs=[ANY] * 2 + [VM] * 5,
        out_specs=[o[1] for o in outs],
        scratch_shapes=[
            pltpu.VMEM((nb, row_blocks, BLK, BLK), F32),
            pltpu.VMEM((nw * BLK, width), BF),
            pltpu.VMEM((3, groups * qkv_own.shape[1], width), BF),
            pltpu.VMEM((nw, width, BLK), BF),
            pltpu.SemaphoreType.DMA((4, 12)),
            pltpu.SemaphoreType.DMA((4, 12)),
            pltpu.SemaphoreType.DMA((2,)),
            pltpu.SemaphoreType.DMA((2,)),
            pltpu.SemaphoreType.DMA((groups - 1,)),
            pltpu.SemaphoreType.DMA((groups - 1,)),
            pltpu.SemaphoreType.DMA((4,)),
        ],
        compiler_params=pltpu.CompilerParams(collective_id=0, has_side_effects=True, vmem_limit_bytes=VMEM_LIMIT),
        name="gather_attend",
    )(tok, qkv_own, out_own, up_own, down_own, vec_own, seg)


def gelu_parts(u):
    bell = jnp.exp(-0.5 * u * u)
    base = 1.0 + (0.3275911 * 0.7071067811865476) * jnp.abs(u)
    t = pl.reciprocal(base, approx=True)
    t = t * (2.0 - base * t)
    poly = t * (0.127414796 + t * (-0.142248368 + t * (0.7107068705 + t * (-0.7265760135 + t * 0.5307027145))))
    tail = poly * bell
    cdf = jnp.where(u >= 0.0, 1.0 - tail, tail)
    return u * cdf, cdf + u * (bell * 0.3989422804014327)


class Sum:
    def __init__(self, n, bits, bufs, sems, at):
        self.n, self.bits, self.at = n, bits, at
        self.mine, self.rc, self.rx, self.ry, self.rz, self.rest = bufs
        self.send, self.recv, self.keep = sems
        r, h = place()
        self.y, self.z = r % 2, (r // 2) % 2
        self.by_x, self.by_c = (r, flip(h, 2)), (r, flip(h, 1))
        self.by_y, self.by_z = (flip(r, 1), h), (flip(r, 2), h)
        self.by_rest = [(flip(r, b), h) for b in bits]

    def copy(self, slot, src, dst, who):
        return remote(src, dst, self.send.at[self.at, slot], self.recv.at[self.at, slot], who)

    def core(self, i):
        return self.copy(i, self.mine.at[0], self.rc.at[i], self.by_c)

    def x(self):
        return self.copy(2, self.mine.at[1], self.rx, self.by_x)

    def half(self, which):
        return pl.ds(pl.multiple_of(which * (self.n // 2), 16), self.n // 2)

    def quarter(self, half, which):
        return pl.ds(pl.multiple_of(half * (self.n // 2) + which * (self.n // 4), 16), self.n // 4)

    def own(self):
        return self.mine.at[2, self.quarter(self.y, self.z), :]

    def landed(self, half, which):
        return self.rx.at[self.quarter(half, which), :]

    def y_down(self):
        return self.copy(3, self.mine.at[2, self.half(1 - self.y), :], self.ry, self.by_y)

    def z_down(self):
        return self.copy(4, self.mine.at[2, self.quarter(self.y, 1 - self.z), :], self.rz, self.by_z)

    def z_up(self):
        return self.copy(5, self.own(), self.landed(self.y, self.z), self.by_z)

    def y_up(self):
        return self.copy(6, self.own(), self.landed(self.y, self.z), self.by_y)

    def y_up2(self):
        return self.copy(7, self.landed(self.y, 1 - self.z), self.landed(self.y, 1 - self.z), self.by_y)

    def swap(self, i):
        return self.copy(8 + i, self.own(), self.rest.at[i], self.by_rest[i])

    def add(self, ref, got):
        ref[...] = (ref[...].astype(F32) + got[...].astype(F32)).astype(BF)

    def c0(self):
        self.core(0).start()

    def f(self):
        self.core(0).wait_recv()
        self.add(self.mine.at[1], self.rc.at[0])

    def xs(self):
        self.x().start()

    def c1(self):
        self.core(1).start()

    def s(self):
        self.core(1).wait_recv()
        self.add(self.mine.at[2], self.rc.at[1])

    def r(self):
        self.x().wait_recv()
        self.add(self.mine.at[2], self.rx)
        self.y_down().start()

    def yy(self):
        self.y_down().wait_recv()
        self.add(self.mine.at[2, self.half(self.y), :], self.ry)
        self.z_down().start()

    def zz(self):
        self.z_down().wait_recv()
        self.add(self.own(), self.rz)
        if self.bits:
            self.swap(0).start()

    def w(self):
        for i in range(len(self.bits)):
            self.swap(i).wait_recv()
            self.swap(i).wait_send()
            self.add(self.own(), self.rest.at[i])
            if i + 1 < len(self.bits):
                self.swap(i + 1).start()
        self.z_up().start()
        self.y_up().start()

    def u(self):
        self.z_up().wait_recv()
        self.y_up2().start()

    def outs(self, out, lo):
        def local(i, src, rows):
            start = pl.multiple_of(lo + rows.start, 16)
            return pltpu.make_async_copy(src, out.at[pl.ds(start, rows.size), :], self.keep.at[self.at, i])

        mine, beside, other = self.quarter(self.y, self.z), self.quarter(self.y, 1 - self.z), self.half(1 - self.y)
        return (
            local(0, self.own(), mine),
            local(1, self.rx.at[beside, :], beside),
            local(2, self.rx.at[other, :], other),
        )

    def e(self, out, lo):
        self.y_up().wait_recv()
        self.y_up2().wait_recv()
        for c in self.outs(out, lo):
            c.start()

    def sent(self, out, lo):
        for c in (self.core(1), self.x(), self.y_down(), self.z_down(), self.z_up(), self.y_up(), self.y_up2()):
            c.wait_send()
        for c in self.outs(out, lo):
            c.wait()


def other_bits(count):
    bits, b = [], 4
    while b < count:
        bits.append(b)
        b *= 2
    return tuple(bits)


def hooks_at(t, plan):
    for at, steps in plan.items():

        @pl.when(t == at)
        def _():
            for step in steps:
                step()


def rest_kernel(
    groups, row_blocks, bits, chunks,
    tok, cot, ctx, ctxt, out_w, up_w, down_w, vec, seg, lse, q_i, k_i, v_i, kt_i, x_i, w_i,
    mixed, o_down, o_up, o_out, o_qkv, o_tok, o_left, o_right, o_vec,
    xhat, inv, g_hid, gx_side, vec_acc, vin, vacc, *scratch,
):
    r, h = place()
    own, width = tok.shape
    nb = own // BLK
    nw = nb + 2 * HALO
    halo = HALO * BLK
    shards = up_w.shape[0]
    all_pairs = q_i.shape[0]
    pairs = all_pairs // 2
    half = pairs * 128
    shard_rows = half // 2
    x_half = (h // 2) % 2
    far_half = 1 - x_half
    core = h % 2
    rows = lambda b: pl.ds(pl.multiple_of(b * BLK, BLK), BLK)
    mean = lambda v: jnp.mean(v, axis=1, keepdims=True)
    gain1, shift1, gain2, shift2 = (vec[i : i + 1, :].astype(F32) for i in range(4))

    n_chunks = len(chunks)
    (send, recv, keep, side_send, side_recv, vsend, vrecv, loc) = scratch[6 * n_chunks :]
    sems = (send, recv, keep)
    outs = {"down": o_down, "up": o_up, "out": o_out, "q": o_qkv.at[0], "k": o_qkv.at[1], "v": o_qkv.at[2]}
    parts = [Sum(n, bits, scratch[6 * i : 6 * i + 6], sems, i) for i, (_, _, n) in enumerate(chunks)]
    by_name = {}
    for part, (name, lo, _) in zip(parts, chunks):
        part.end = functools.partial(part.e, outs[name], lo)
        part.done = functools.partial(part.sent, outs[name], lo)
        by_name.setdefault(name, []).append(part)
    downs, ups, (out_c,) = by_name["down"], by_name["up"], by_name["out"]
    q_c, k_c, v_c = (by_name[name][0] for name in "qkv")
    one = parts[0]

    def shard_of(i):
        across = 1 - i // 2
        other = 1 - i % 2
        return h + across * (2 - 4 * x_half) + other * (1 - 2 * core)

    def slot_of(i):
        return (i % 2) * (1 + i // 2)

    def fetch(src, dst, i):
        return pltpu.make_async_copy(src, dst, loc.at[i])

    vec_ids = [one.by_c, one.by_x, one.by_y, one.by_z] + one.by_rest

    def vstep(i):
        src = vec_acc if i == 0 else vacc.at[i - 1]
        return remote(src, vin.at[i], vsend.at[i], vrecv.at[i], vec_ids[i])

    def vnext(i):
        vstep(i).wait_recv()
        vacc[i] = (vec_acc[...] if i == 0 else vacc[i - 1]) + vin[i]
        if i + 1 < len(vec_ids):
            vstep(i + 1).start()

    def dense(tok_v, cot_v, ctx_v, out_v, up_v, down_v, mix_v, hl, ht, ffn, act_t, slope, g_low, gup):
        first = [fetch(a, b, i) for i, (a, b) in enumerate(((tok, tok_v), (ctx, ctx_v), (out_w, out_v), (cot, cot_v)))]
        for c in first:
            c.start()

        def weights(s, slot):
            return fetch(up_w.at[s], up_v.at[slot], 4 + slot), fetch(down_w.at[s], down_v.at[slot], 6 + slot)

        def start_weights(s, slot):
            for c in weights(s, slot):
                c.start()

        def wait_weights(s, slot):
            for c in weights(s, slot):
                c.wait()

        for i in range(2):
            start_weights(shard_of(3 - i), i)
        greet(group_of(r, h, groups) + [one.by_y, one.by_z] + one.by_rest)
        vec_acc[...] = jnp.zeros_like(vec_acc)
        for c in first:
            c.wait()

        def before(b, c):
            resid = tok_v[rows(b), :].astype(F32) + nn(ctx_v[rows(b), :], out_v[...])
            cen = resid - mean(resid)
            rs = lax.rsqrt(mean(cen * cen) + NORM_EPS)
            n = cen * rs
            hidden = n * gain1 + shift1
            xhat[rows(b), :] = n
            inv[rows(b), :] = jnp.broadcast_to(rs, (BLK, 128))
            low = hidden.astype(BF)
            hl[rows(b), :] = low
            ht[b] = low.T
            ffn[rows(b), :] = hidden
            return c

        lax.fori_loop(0, nb, before, 0)

        def forward(i, c):
            s, slot = shard_of(3 - i), i % 2
            wait_weights(s, slot)

            def one_block(b, cc):
                up = nn(hl[rows(b), :], up_v[slot])
                active, deriv = gelu_parts(up)
                active = active.astype(BF)
                slope[s, rows(b), :] = deriv.astype(BF)
                act_t[s, b] = active.T
                ffn[rows(b), :] += nn(active, down_v[slot])
                return cc

            lax.fori_loop(0, nb, one_block, 0)

            @pl.when(i + 2 < shards)
            def _():
                start_weights(shard_of(1 - i), slot)

            return c

        lax.fori_loop(0, shards, forward, 0)

        def middle(b, c):
            v = ffn[rows(b), :]
            cen = v - mean(v)
            rs = lax.rsqrt(mean(cen * cen) + NORM_EPS)
            n = cen * rs
            mix_v[rows(b), :] = (n * gain2 + shift2).astype(BF)
            ct = cot_v[rows(b), :].astype(F32)
            vec_acc[2:3, :] += jnp.sum(ct * n, axis=0, keepdims=True)
            vec_acc[3:4, :] += jnp.sum(ct, axis=0, keepdims=True)
            e = ct * gain2
            g = rs * (e - mean(e) - n * mean(e * n))
            g_hid[rows(b), :] = g
            g_low[rows(b), :] = g.astype(BF)
            return c

        lax.fori_loop(0, nb, middle, 0)
        mix_out = fetch(mix_v, mixed, 0)
        mix_out.start()

        def grad_rows(left, right, part, part_i, slot):
            n = part.n
            acc = jnp.zeros((n, width), F32)
            for b in range(nb):
                acc += nn(left(b, pl.ds(part_i * n, n)), right[b * BLK : (b + 1) * BLK, :])
            part.mine[slot] = acc.astype(BF)

        def down_grads(i, c):
            s, slot = shard_of(i), slot_of(i)

            @pl.when(i == 2)
            def _():
                for p in downs:
                    p.core(0).wait_send()

            for k, p in enumerate(downs):
                grad_rows(lambda b, n: act_t[s, b, n, :], g_low, p, k, slot)
            hooks_at(i, {
                0: [p.c0 for p in downs],
                1: [f for p in downs for f in (p.f, p.xs)],
                2: [p.c1 for p in downs],
                3: [p.s for p in downs],
            })
            return c

        lax.fori_loop(0, shards, down_grads, 0)

        def backward(i, c):
            s, slot = shard_of(i), 1 - i % 2

            @pl.when(i >= 2)
            def _():
                wait_weights(s, slot)

            def one_block(b, cc):
                ga = nt(g_low[rows(b), :], down_v[slot])
                gu = (slope[s, rows(b), :].astype(F32) * ga).astype(BF)
                gup[rows(b), :] = gu
                g_hid[rows(b), :] += nt(gu, up_v[slot])
                return cc

            lax.fori_loop(0, nb, one_block, 0)

            @pl.when(i < 2)
            def _():
                start_weights(shard_of(i + 2), slot)

            @pl.when(i == 2)
            def _():
                for p in ups:
                    p.core(0).wait_send()

            for k, p in enumerate(ups):
                grad_rows(lambda b, n: ht[b, n, :], gup, p, k, slot_of(i))
            hooks_at(i, {
                0: [p.c0 for p in ups],
                1: [p.f for p in ups],
                2: [p.c1 for p in ups],
                3: [p.s for p in ups] + [f for d, p in zip(downs, ups) for f in (d.r, p.xs)],
            })
            return c

        lax.fori_loop(0, shards, backward, 0)
        mix_out.wait()

    pl.run_scoped(
        dense,
        *[pltpu.VMEM((own, width), BF)] * 4,
        pltpu.VMEM((2, width, width), BF),
        pltpu.VMEM((2, width, width), BF),
        pltpu.VMEM((own, width), BF),
        pltpu.VMEM((own, width), BF),
        pltpu.VMEM((nb, width, BLK), BF),
        pltpu.VMEM((own, width), F32),
        pltpu.VMEM((shards, nb, width, BLK), BF),
        pltpu.VMEM((shards, own, width), BF),
        pltpu.VMEM((own, width), BF),
        pltpu.VMEM((own, width), BF),
    )

    def attention(q_v, g_v, x_v, w_v, k_v, v_v, kt_v, delta, bias, dk, dv, dqt, dkt, dvt):
        def keys(hf):
            base = pl.multiple_of(hf * half, 128)
            return (
                fetch(k_i.at[pl.ds(hf * pairs, pairs)], k_v, 0),
                fetch(v_i.at[pl.ds(hf * pairs, pairs)], v_v, 1),
                fetch(kt_i.at[:, pl.ds(base, half), :], kt_v, 2),
            )

        q_in, x_in, w_in = fetch(q_i, q_v, 3), fetch(x_i, x_v, 4), fetch(w_i, w_v, 5)
        for c in (*keys(far_half), q_in, x_in, w_in):
            c.start()

        def between(out_v, ctxt_v, low_v):
            o_in, c_in = fetch(out_w, out_v, 6), fetch(ctxt, ctxt_v, 7)
            o_in.start()
            c_in.start()
            o_in.wait()
            c_in.wait()

            def after(b, c):
                g = g_hid[rows(b), :]
                n = xhat[rows(b), :]
                vec_acc[0:1, :] += jnp.sum(g * n, axis=0, keepdims=True)
                vec_acc[1:2, :] += jnp.sum(g, axis=0, keepdims=True)
                e = g * gain1
                res = inv[rows(b), 0:1] * (e - mean(e) - n * mean(e * n))
                g_hid[rows(b), :] = res
                low = res.astype(BF)
                low_v[rows(b), :] = low
                gc = nt(low, out_v[...]).astype(BF)
                for i in range(all_pairs):
                    g_v[i, rows(b), :] = gc[:, i * 128 : (i + 1) * 128]
                prod = nt(out_v[...], low).astype(BF).astype(F32) * ctxt_v[b]
                for i in range(2 * all_pairs):
                    delta[b, i] = jnp.sum(prod[i * HEAD_WIDTH : (i + 1) * HEAD_WIDTH, :], axis=0, keepdims=True)
                return c

            lax.fori_loop(0, nb, after, 0)
            vstep(0).start()
            downs[0].yy()

            def grad_out(i, c):
                @pl.when(i == 2)
                def _():
                    out_c.core(0).wait_send()

                base = pl.multiple_of(shard_of(i) * shard_rows, 16)
                acc = jnp.zeros((shard_rows, width), F32)
                for b in range(nb):
                    acc += nn(ctxt_v[b, pl.ds(base, shard_rows), :].astype(BF), low_v[b * BLK : (b + 1) * BLK, :])
                out_c.mine[slot_of(i)] = acc.astype(BF)
                hooks_at(i, {0: [out_c.c0], 1: [out_c.f], 2: [out_c.c1], 3: [out_c.s]})
                return c

            lax.fori_loop(0, shards, grad_out, 0)
            downs[1].yy()
            downs[0].zz()

        pl.run_scoped(
            between,
            pltpu.VMEM((width, width), BF),
            pltpu.VMEM((nb, width, BLK), F32),
            pltpu.VMEM((own, width), BF),
        )
        q_in.wait()

        def unit(hf, t):
            j, i = t // pairs, t % pairs
            p = hf * pairs + i
            ws = window_start(h, j, nb, row_blocks)

            @pl.when(i == 0)
            def _():
                for kb in range(row_blocks):
                    bias[kb] = mask_of(seg[ws + kb], seg[HALO + j])

            q = q_v[p, rows(j), :]
            g = g_v[p, rows(j), :]
            lane = lax.broadcasted_iota(jnp.int32, q.shape, 1)
            qm = [jnp.where(lane // HEAD_WIDTH == hh, q, jnp.zeros_like(q)) for hh in range(2)]
            gm = [jnp.where(lane // HEAD_WIDTH == hh, g, jnp.zeros_like(g)) for hh in range(2)]
            acc = [jnp.zeros((HEAD_WIDTH, BLK), F32) for _ in range(2)]
            for kb in range(row_blocks):
                kblk = k_v[i, rows(ws + kb), :]
                vblk = v_v[i, rows(ws + kb), :]
                add_k = None
                for hh in range(2):
                    head = 2 * p + hh
                    s = nt(kblk, qm[hh]) + bias[kb]
                    prob = jnp.exp(s - lse[j, head])
                    gp = nt(vblk, gm[hh])
                    gs = (prob * (gp - delta[j, head])).astype(BF)
                    one_v = nn(prob.astype(BF), gm[hh])
                    one_k = nn(gs, qm[hh])
                    add_k, add_v = (one_k, one_v) if add_k is None else (add_k + one_k, add_v + one_v)
                    at = pl.multiple_of((2 * i + hh) * HEAD_WIDTH, HEAD_WIDTH)
                    acc[hh] += nn(kt_v[ws + kb, pl.ds(at, HEAD_WIDTH), :], gs)
                dk[i, rows(ws + kb), :] += add_k
                dv[i, rows(ws + kb), :] += add_v
            for hh in range(2):
                at = pl.multiple_of((2 * i + hh) * HEAD_WIDTH, HEAD_WIDTH)
                dqt[j, pl.ds(at, HEAD_WIDTH), :] = (acc[hh] * HEAD_WIDTH**-0.5).astype(BF)

        def attend_half(hf, plan):
            dk[...] = jnp.zeros_like(dk)
            dv[...] = jnp.zeros_like(dv)

            def body(t, c):
                hooks_at(t, plan)
                unit(hf, t)
                return c

            lax.fori_loop(0, nb * pairs, body, 0)
            for b in range(nw):
                lo, hi = b * BLK, (b + 1) * BLK
                dkt[b] = jnp.concatenate([dk[p, lo:hi, :].astype(BF) for p in range(pairs)], axis=1).T
                dvt[b] = jnp.concatenate([dv[p, lo:hi, :].astype(BF) for p in range(pairs)], axis=1).T

        def weight_grads(which, slot):
            at = pl.multiple_of(which * shard_rows, 16)
            acc = jnp.zeros((shard_rows, width), F32)
            for j in range(nb):
                acc += nn(dqt[j, pl.ds(at, shard_rows), :], x_v[(HALO + j) * BLK : (HALO + j + 1) * BLK, :])
            q_c.mine[slot] = acc.astype(BF)
            for c, src in ((k_c, dkt), (v_c, dvt)):
                acc = jnp.zeros((shard_rows, width), F32)
                for b in range(nw):
                    acc += nn(src[b, pl.ds(at, shard_rows), :], x_v[b * BLK : (b + 1) * BLK, :])
                c.mine[slot] = acc.astype(BF)

        def input_grads(hf, last):
            base = pl.multiple_of(hf * half, 128)
            wk, wv = w_v.at[1, pl.ds(base, half), :], w_v.at[2, pl.ds(base, half), :]

            def block(b):
                kb = jnp.concatenate([dk[p, rows(b), :].astype(BF) for p in range(pairs)], axis=1)
                vb = jnp.concatenate([dv[p, rows(b), :].astype(BF) for p in range(pairs)], axis=1)
                return nn(kb, wk[...]) + nn(vb, wv[...])

            def side(i, c):
                b = i + jnp.where(i >= HALO, nb, 0)
                total = block(b)
                if last:
                    total = total + gx_side[rows(i), :].astype(F32)
                gx_side[rows(i), :] = total.astype(BF)
                return c

            lax.fori_loop(0, 2 * HALO, side, 0)

            def inner(j, c):
                g_hid[rows(j), :] += block(j + HALO) + nn(dqt[j].T, w_v[0, pl.ds(base, half), :])
                return c

            return lambda: lax.fori_loop(0, nb, inner, 0)

        for c in keys(far_half):
            c.wait()
        d0, d1 = downs
        u0, u1 = ups
        attend_half(far_half, {
            1: [d1.zz], 2: [d0.w], 3: [d1.w], 5: [d0.u, d1.u],
            7: [u0.r, u1.r, out_c.xs], 8: [d0.end, d1.end],
        })
        for c in keys(x_half):
            c.start()
        x_in.wait()
        w_in.wait()
        weight_grads(1 - core, 0)
        for p in (q_c, k_c, v_c):
            p.c0()
        weight_grads(core, 1)
        for p in (q_c, k_c, v_c):
            p.f()
            p.xs()
        u0.yy()
        u1.yy()
        input_grads(far_half, False)()
        u0.zz()
        u1.zz()
        out_c.r()
        for c in keys(x_half):
            c.wait()
        attend_half(x_half, {
            0: [lambda: vnext(0)], 1: [u0.w, lambda: vnext(1)], 2: [u1.w, out_c.yy, lambda: vnext(2)], 3: [out_c.zz, lambda: vnext(3)],
            4: [u0.u, u1.u], 5: [out_c.w], 6: [u0.end, u1.end, out_c.u], 7: [out_c.end],
            8: [functools.partial(vnext, i) for i in range(4, len(vec_ids))],
        })
        for p in (q_c, k_c, v_c):
            p.core(0).wait_send()
        weight_grads(1 - core, 0)
        for p in (q_c, k_c, v_c):
            p.c1()
        weight_grads(core, 2)
        for p in (q_c, k_c, v_c):
            p.s()
            p.r()
        finish = input_grads(x_half, True)

        @pl.when(h > 0)
        def _():
            to_left.start()

        @pl.when(h < groups - 1)
        def _():
            to_right.start()

        for p in (q_c, k_c, v_c):
            p.yy()
        for p in (q_c, k_c, v_c):
            p.zz()
        finish()
        tok_out = fetch(g_hid, o_tok, 3)
        tok_out.start()
        for p in (q_c, k_c, v_c):
            p.w()
        for p in (q_c, k_c, v_c):
            p.u()
        for p in (q_c, k_c, v_c):
            p.end()
        tok_out.wait()

    to_left = remote(gx_side.at[pl.ds(0, halo), :], o_right, side_send.at[0], side_recv.at[0], (r, h - 1))
    to_right = remote(gx_side.at[pl.ds(halo, halo), :], o_left, side_send.at[1], side_recv.at[1], (r, h + 1))

    pl.run_scoped(
        attention,
        pltpu.VMEM((all_pairs, own, 128), BF),
        pltpu.VMEM((all_pairs, own, 128), BF),
        pltpu.VMEM((nw * BLK, width), BF),
        pltpu.VMEM((3, width, width), BF),
        pltpu.VMEM((pairs, nw * BLK, 128), BF),
        pltpu.VMEM((pairs, nw * BLK, 128), BF),
        pltpu.VMEM((nw, half, BLK), BF),
        pltpu.VMEM((nb, 2 * all_pairs, 1, BLK), F32),
        pltpu.VMEM((row_blocks, BLK, BLK), F32),
        pltpu.VMEM((pairs, nw * BLK, 128), F32),
        pltpu.VMEM((pairs, nw * BLK, 128), F32),
        pltpu.VMEM((nb, half, BLK), BF),
        pltpu.VMEM((nw, half, BLK), BF),
        pltpu.VMEM((nw, half, BLK), BF),
    )

    o_vec[...] = vacc[len(vec_ids) - 1]
    for p in parts:
        p.done()
    for i in range(len(vec_ids)):
        vstep(i).wait_send()

    @pl.when(h > 0)
    def _():
        to_left.wait_send()
        to_right.wait_recv()

    @pl.when(h == 0)
    def _():
        gx_side[pl.ds(0, halo), :] = jnp.zeros((halo, width), BF)
        pltpu.sync_copy(gx_side.at[pl.ds(0, halo), :], o_left)

    @pl.when(h < groups - 1)
    def _():
        to_right.wait_send()
        to_left.wait_recv()

    @pl.when(h == groups - 1)
    def _():
        gx_side[pl.ds(halo, halo), :] = jnp.zeros((halo, width), BF)
        pltpu.sync_copy(gx_side.at[pl.ds(halo, halo), :], o_right)


def rest(groups, row_blocks, row_devices, tok, cot, ctx, ctxt, out_w, up_w, down_w, vec, seg, lse, q, k, v, kt, x, w):
    own, width = tok.shape
    shard_rows = width // groups
    nb = own // BLK
    bits = other_bits(row_devices)
    split = width // 2
    chunks = [(name, lo, split) for name in ("down", "up") for lo in range(0, width, split)]
    chunks += [(name, 0, shard_rows) for name in ("out", "q", "k", "v")]
    hops = 4 + len(bits)
    scratch = [
        pltpu.VMEM((own, width), F32),
        pltpu.VMEM((own, 128), F32),
        pltpu.VMEM((own, width), F32),
        pltpu.VMEM((2 * HALO * BLK, width), BF),
        pltpu.VMEM((8, width), F32),
        pltpu.VMEM((hops, 8, width), F32),
        pltpu.VMEM((hops, 8, width), F32),
    ]
    for _, _, n in chunks:
        scratch += [
            pltpu.VMEM((3, n, width), BF),
            pltpu.VMEM((2, n, width), BF),
            pltpu.VMEM((n, width), BF),
            pltpu.VMEM((n // 2, width), BF),
            pltpu.VMEM((n // 4, width), BF),
            pltpu.VMEM((max(1, len(bits)), n // 4, width), BF),
        ]
    scratch += [
        pltpu.SemaphoreType.DMA((len(chunks), 8 + len(bits))),
        pltpu.SemaphoreType.DMA((len(chunks), 8 + len(bits))),
        pltpu.SemaphoreType.DMA((len(chunks), 3)),
        pltpu.SemaphoreType.DMA((2,)),
        pltpu.SemaphoreType.DMA((2,)),
        pltpu.SemaphoreType.DMA((hops,)),
        pltpu.SemaphoreType.DMA((hops,)),
        pltpu.SemaphoreType.DMA((8,)),
    ]
    s = jax.ShapeDtypeStruct
    side = s((HALO * BLK, width), BF)
    outs = [
        (s((own, width), BF), ANY),
        (s((width, width), BF), ANY),
        (s((width, width), BF), ANY),
        (s((shard_rows, width), BF), ANY),
        (s((3, shard_rows, width), BF), ANY),
        (s((own, width), F32), ANY),
        (side, ANY),
        (side, ANY),
        (s((8, width), F32), VM),
    ]
    return pl.pallas_call(
        functools.partial(rest_kernel, groups, row_blocks, bits, chunks),
        out_shape=[o[0] for o in outs],
        in_specs=[ANY] * 7 + [VM] * 3 + [ANY] * 6,
        out_specs=[o[1] for o in outs],
        scratch_shapes=scratch,
        compiler_params=pltpu.CompilerParams(collective_id=1, has_side_effects=True, vmem_limit_bytes=VMEM_LIMIT),
        name="rest",
    )(tok, cot, ctx, ctxt, out_w, up_w, down_w, vec, seg, lse, q, k, v, kt, x, w)


def local(
    groups, row_devices,
    tokens, lengths, w_query, w_key, w_value, w_out, w_up, w_down,
    gain_first, shift_first, gain_second, shift_second, cotangent,
):
    packed_rows = lengths.shape[0]
    own, width = tokens.shape
    row_length = groups * own // packed_rows
    row_blocks = row_length // BLK
    nw = own // BLK + 2 * HALO
    h = lax.axis_index("heads")

    n_vec = gain_first.shape[0]
    vec_own = jnp.pad(jnp.stack([gain_first, shift_first, gain_second, shift_second]), ((0, 12), (0, -n_vec % 128)))
    doc_ends = jnp.cumsum(lengths, axis=1)
    position = lax.broadcasted_iota(jnp.int32, (packed_rows, row_length, lengths.shape[1]), 1)
    span = jnp.sum((position >= doc_ends[:, None, :]).astype(jnp.int32), axis=2)
    ids = span + lengths.shape[1] * lax.broadcasted_iota(jnp.int32, span.shape, 0)
    ids = jnp.pad(ids.reshape(-1), (HALO * BLK, HALO * BLK), constant_values=-1)
    seg = lax.dynamic_slice(ids, (own * h,), (nw * BLK,)).reshape(nw, 1, BLK)

    qkv_own = jnp.stack([w_query.T, w_key.T, w_value.T])
    shard_cols = w_up.shape[1]
    (qkv, out_w, up_w, down_w, vec_all, x_win, q, k, v, kt, ctx, ctxt, lse) = gather_attend(
        groups, row_blocks, tokens, qkv_own, w_out[None], w_up[None], w_down[None], vec_own, seg
    )
    vec = vec_all[:, :4, :n_vec].transpose(1, 0, 2).reshape(4, width)
    up_w = up_w.reshape(groups, width, shard_cols)
    down_w = down_w.reshape(groups, shard_cols, width)
    mixed, o_down, o_up, o_out, o_qkv, gx, gx_left, gx_right, o_vec = rest(
        groups, row_blocks, row_devices, tokens, cotangent, ctx, ctxt, out_w[0], up_w, down_w, vec,
        seg, lse, q, k, v, kt, x_win, qkv,
    )
    halo = HALO * BLK
    o_tok = gx + jnp.pad(gx_left.astype(F32), ((0, own - halo), (0, 0))) + jnp.pad(gx_right.astype(F32), ((own - halo, 0), (0, 0)))
    mine = lax.dynamic_slice(o_vec, (0, n_vec * h), (4, n_vec))
    wide = lambda a: a.astype(F32)
    return (
        mixed, o_tok, wide(o_qkv[0].T), wide(o_qkv[1].T), wide(o_qkv[2].T), wide(o_out), wide(o_up), wide(o_down),
        mine[0], mine[1], mine[2], mine[3],
    )


def solution(mesh):
    both, heads = P(("rows", "heads"), None), P("heads")
    cols, rows = P(None, "heads"), P("heads", None)
    return jax.shard_map(
        functools.partial(local, mesh.shape["heads"], mesh.shape["rows"]),
        mesh=mesh,
        in_specs=(both, P("rows", None), cols, cols, cols, rows, cols, rows, heads, heads, heads, heads, both),
        out_specs=(both, both, cols, cols, cols, rows, cols, rows, heads, heads, heads, heads),
        check_vma=False,
    )
```

time: 389 us -> 288 us (0.74)
  Pallas kernels: 365 us -> 266 us
  other arithmetic: 3.24 us -> 12.9 us
  local copies, waits for them, and re-layouts: 13.9 us -> 7.38 us
  blocking collectives: 5.35 us -> 0 us
    pallas_call x3 -> x1, Pallas kernels: 265 us -> 194 us  [rest(): pl.pallas_call(functools.partial(rest_kernel, groups, row_blocks, bits, c...]
    pallas_call x1, Pallas kernels: 100 us -> 72.6 us  [gather_attend(): pl.pallas_call(functools.partial(gather_attend_kernel, groups, row_blocks...]
    unnamed x21 -> x11, local copies, waits for them, and re-layouts: 7.54 us -> 1.12 us
    all_gather x1 -> x0, blocking collectives: 5.35 us -> none  [local(): lax.all_gather(jnp.stack([gain_first, shift_first, gain_second, shift_sec...]
    convert_element_type x0 -> x4, other arithmetic: none -> 5.25 us  [local(): wide = lambda a: a.astype(F32)]
where the time goes in v2:
time: 288 us; the launch traced here: 287 us
  Pallas kernels  266 us (92%)
  other arithmetic  12.9 us (4%)
  local copies, waits for them, and re-layouts  7.38 us (3%)
    pallas_call x1, Pallas kernels, rest(): pl.pallas_call(functools.partial(rest_kernel, groups, row_blocks, bits, c...  194 us
    pallas_call x1, Pallas kernels, gather_attend(): pl.pallas_call(functools.partial(gather_attend_kernel, groups, row_blocks...  72.6 us

profile of v2, /device:TPU:0, one launch (start us, length us, event | category | flops | bytes accessed | tf_op | source)
XLA Modules:
  0.0 287.4 jit_solution(269412091705407749)
XLA Ops:
  0.6 0.9 reduce_window_sum.11
  1.5 0.1 convert_reduce_fusion
  1.7 0.1 broadcast_add_fusion
  1.8 0.1 pad_dynamic-slice_fusion
  1.8 0.6 reshape.49.seg
  2.4 2.1 pad_maximum_fusion.qkv_own
  4.6 0.7 stack.31
  5.3 0.7 stack.32
  5.9 0.7 stack.33
  6.6 0.7 stack.34
  7.2 0.6 fusion.8.vec_own
  7.8 72.6 %gather_attend.1 = (bf16[3,768,768]{2,1,0:T(8,128)(2,1)}, bf16[1,768,768]{2,1,0:T(8,128)(2,1)}, bf16[1,3072,768]{2,1,0:T(8,128)(2,1)}, bf16[1,3072,768]{2,1,0:T(...) custom-call(bf16[768,768]{1,0:T(8,128)(2,1)} %tok.3, ...), custom_call_target="tpu_custom_call" | custom-call | tf_op jit(solution)/shard_map/gather_attend/pallas_call | solution.py:382
  80.5 0.7 slice_bitcast_fusion
  81.2 0.7 reshape.52.vec
  81.9 193.8 %rest.1 = (bf16[768,768]{1,0:T(8,128)(2,1)}, bf16[768,768]{1,0:T(8,128)(2,1)}, bf16[768,768]{1,0:T(8,128)(2,1)}, bf16[192,768]{1,0:T(8,128)(2,1)}, bf16[3,192,76...) custom-call(bf16[768,768]{1,0:T(8,128)(2,1)} %tok.3, ...), custom_call_target="tpu_custom_call" | custom-call | tf_op jit(solution)/shard_map/rest/pallas_call | solution.py:1099
  275.7 0.0 copy-start.1
  275.7 3.8 %convert_add_fusion = f32[768,768]{1,0:T(8,128)} fusion(f32[768,768]{1,0:T(8,128)} %get-tuple-element.48, bf16[512,768]{1,0:T(8,128)(2,1)} %get-tuple-element.50, bf16[512,768]{1,0:T(8,128)(2,1)} %get-tuple-element.49), kind=kLoop, calls=%fused_computation | loop fusion | flops 2359296 | bytes 6291456 | tf_op jit(solution)/shard_map/add | solution.py:1144
  279.5 0.0 copy-start
  279.5 0.0 copy-done.1
  279.5 1.6 convert_element_type.58
  281.1 0.0 copy-start.3
  281.1 0.1 copy-done
  281.2 0.0 copy-start.4
  281.2 1.6 convert_element_type.59
  282.8 0.0 copy-start.2
  282.8 0.0 copy-done.3
  282.8 1.2 convert_bitcast_fusion
  284.0 0.0 copy-done.4
  284.0 0.9 convert_element_type.57
  284.9 1.5 fusion.12
  286.4 0.0 copy-done.2
  286.4 1.0 copy.28
  (3 shorter events, 0.0 us)
Async XLA Ops:
  275.7 3.8 %copy-start.1 = (bf16[768,768]{1,0:T(8,128)(2,1)S(1)}, bf16[768,768]{1,0:T(8,128)(2,1)}, u32[]{:S(2)}) copy-start(bf16[768,768]{1,0:T(8,128)(2,1)} %get-tuple-element.53) | copy-start | bytes 3538948
  279.5 1.7 copy-start
  281.1 1.7 copy-start.3
  281.2 2.8 copy-start.4
  282.8 3.6 %copy-start.2 = (bf16[768,768]{1,0:T(8,128)(2,1)S(1)}, bf16[768,768]{1,0:T(8,128)(2,1)}, u32[]{:S(2)}) copy-start(bf16[768,768]{1,0:T(8,128)(2,1)} %get-tuple-element.75) | copy-start | bytes 3538948
